TPU v7x, 256 devices: a whole 4x4x8 slice. The times are simulated.
256 devices in a mesh: bin: 8 (over z_hi, x), slab: 32 (over z_lo, y, core).
Axes of the slice: x: 4, y: 4, z: 8 (z_hi: 2, z_lo: 4; z = z_hi * 4 + z_lo), core: 2. Of those that a mesh axis runs over, the one named last changes fastest.
Arguments:
- sample_data: bfloat16 [8192, 2048], P(('bin', 'slab')), may hold values from -6 to 6
- block_route: int32 [8192, 1], P(('bin', 'slab')), may hold values from 0 to 23, as said below
- spoke_index: int32 [8192], P(('bin', 'slab')), may hold values from 0 to 32767
- segment_index: int32 [8192], P(('bin', 'slab')), may hold values from 0 to 11
- sample_count: int32 [8192], P(('bin', 'slab')), may hold values from 16 to 32
- sensitivity: bfloat16 [96, 262144], P(None, 'slab'), may hold values from -6 to 6
- image: float32 [8, 96, 8192], P('bin', None, 'slab'), may hold values from -6 to 6
- tv_weight: float32 [8, 96, 4096], P('bin', None, 'slab'), may hold values from 0.3 to 3
Outputs:
- gradient: float32 [8, 96, 8192], P('bin', None, 'slab')
Inputs may be any that keep to these rules, and one draw needn't show every extreme that they name: `block_route`: among the 32 blocks of one device no value occurs more than 4 times; for every slab index one value occurs exactly 4 times on every device with that slab index.
All inputs are finite; a program needn't handle non-finite values.
Results may differ from a plain program's by a relative error of at most 0.0037.
Values may be sent and summed in bfloat16 or wider, within the bound.
A program may use at most 128 MiB of HBM per device.

v0:
```python
import math

import jax
import jax.numpy as jnp
from jax import lax
from jax.sharding import PartitionSpec as P

C = 32
NG = 384
NXI = 256
WY = 16
RO = 384
P_SIZE = 32
R = 40
KP = 3
BLKB = 4
CAPK = 4


SMOOTHING = 0.5
GOLDEN_STEP = 40503
TURN_STEPS = 65536


def from_behind(shard, axis, by):
    peers = lax.axis_size(axis)
    pairs = [(i, i + by) for i in range(peers) if 0 <= i + by < peers]
    return lax.ppermute(shard, axis, pairs)


def spline_weight(offset):
    distance = jnp.abs(offset)
    inside = 2.0 / 3.0 - distance * distance + 0.5 * distance * distance * distance
    outside = jnp.maximum(2.0 - distance, 0.0) ** 3 / 6.0
    return jnp.where(distance < 1.0, inside, outside)


def phase_table(out_index, input_index, modulus):
    turn_index = out_index[:, None] * input_index[None, :] % modulus
    angles = 2.0 * math.pi / modulus * turn_index.astype(jnp.float32)
    return jnp.concatenate([jnp.cos(angles), jnp.sin(angles)], axis=0).astype(jnp.bfloat16)


def sample_coords(spoke_ids, segment, samples, readout, grid):
    fraction = (spoke_ids * GOLDEN_STEP % TURN_STEPS).astype(jnp.float32) / TURN_STEPS
    angles = 2.0 * math.pi * fraction
    sample_step = jnp.arange(samples, dtype=jnp.int32)
    radial = (
        (segment[:, None] * samples + sample_step[None, :] - readout // 2).astype(jnp.float32) + 0.5
    ) * ((grid - 8) / readout)
    coord_x = grid / 2 + radial * jnp.cos(angles)[:, None]
    coord_y = grid / 2 + radial * jnp.sin(angles)[:, None]
    return (coord_x, coord_y)


def tile_lines(data, spoke_ids, segment, counts, samples, readout, grid, tile, rows, coils):
    tile_count = data.shape[0]
    coord_x, coord_y = sample_coords(spoke_ids, segment, samples, readout, grid)
    sample_step = jnp.arange(samples, dtype=jnp.int32)
    usable = (sample_step[None, :] < counts[:, None]).astype(jnp.float32)
    tile_start = (jnp.floor(jnp.min(coord_x, axis=1)) - 2.0).astype(jnp.int32)
    columns = tile_start[:, None] + jnp.arange(tile, dtype=jnp.int32)[None, :]
    across_bins = (
        spline_weight(coord_x[:, :, None] - columns[:, None, :].astype(jnp.float32))
        * usable[:, :, None]
    )
    tap_cells = (jnp.floor(coord_y).astype(jnp.int32) - 1)[:, :, None] + jnp.arange(
        4, dtype=jnp.int32
    )[None, None, :]
    tap_weight = spline_weight(coord_y[:, :, None] - tap_cells.astype(jnp.float32))
    row_start_offsets = jnp.arange(rows, dtype=jnp.int32) - rows // 2
    turn_index = (
        row_start_offsets[None, None, None, :] * (tap_cells[:, :, :, None] - grid // 2) % grid
    )
    angles = 2.0 * math.pi / grid * turn_index.astype(jnp.float32)
    real_weight = jnp.sum(tap_weight[:, :, :, None] * jnp.cos(angles), axis=2)
    imag_weight = jnp.sum(tap_weight[:, :, :, None] * jnp.sin(angles), axis=2)
    values = data.astype(jnp.float32).reshape(tile_count, samples, 2, coils)
    data_real = values[:, :, 0, :, None]
    data_imag = values[:, :, 1, :, None]
    real_part = real_weight[:, :, None, :] * data_real - imag_weight[:, :, None, :] * data_imag
    imag_part = real_weight[:, :, None, :] * data_imag + imag_weight[:, :, None, :] * data_real
    weighted_values = jnp.stack([real_part, imag_part], axis=2).astype(jnp.bfloat16)
    weighted_values = weighted_values.reshape(tile_count, samples, 2 * coils * rows)
    return (across_bins.astype(jnp.bfloat16), weighted_values, columns % grid)


def combine_coils(transformed, maps, columns, coils, rows):
    kz_depth = maps.shape[0]
    halves = transformed.reshape(2, kz_depth, columns, 2, coils, rows)
    sens_values = maps.astype(jnp.float32).reshape(kz_depth, columns, 2, coils, rows)
    image_real = halves[0, :, :, 0] - halves[1, :, :, 1]
    image_imag = halves[0, :, :, 1] + halves[1, :, :, 0]
    sens_real = sens_values[:, :, 0]
    sens_imag = sens_values[:, :, 1]
    out_real = jnp.sum(sens_real * image_real + sens_imag * image_imag, axis=2)
    out_imag = jnp.sum(sens_real * image_imag - sens_imag * image_real, axis=2)
    return jnp.stack([out_real, out_imag], axis=2)


def edge_flux(lower_image, upper_image, weight):
    difference = upper_image - lower_image
    magnitude = jnp.sqrt(jnp.sum(difference * difference, axis=-2) + SMOOTHING * SMOOTHING)
    return weight[..., None, :] * difference / magnitude[..., None, :]


def slot_positions(routes, key_count):
    hits = (routes[:, None] == jnp.arange(key_count, dtype=jnp.int32)[None, :]).astype(jnp.int32)
    earlier = jnp.cumsum(hits, axis=0) - hits
    ranking = jnp.sum(earlier * hits, axis=1)
    return routes * CAPK + ranking


def place_tags(tags, placed, slot_count):
    return jnp.zeros((slot_count,), jnp.int32).at[placed].set(tags)


def shards(
    sample_data,
    block_route,
    spoke_index,
    segment_index,
    sample_count,
    sensitivity,
    image,
    tv_weight,
):
    bin_count = lax.axis_size("bin")
    slab_count = lax.axis_size("slab")
    my_bin = lax.axis_index("bin")
    features = 2 * C * WY
    key_count = bin_count * KP
    slot_count = key_count * CAPK
    per_bin = KP * CAPK
    routes = block_route[:, 0]
    placed = slot_positions(routes, key_count)
    outgoing = jnp.zeros((slot_count, P_SIZE * 2 * C), jnp.bfloat16).at[placed].set(sample_data)
    arrived = lax.all_to_all(
        outgoing.reshape(bin_count, per_bin, P_SIZE * 2 * C),
        "bin",
        split_axis=0,
        concat_axis=0,
        tiled=True,
    )
    spoke_out = place_tags(spoke_index, placed, slot_count).reshape(bin_count, per_bin)
    segment_out = place_tags(segment_index, placed, slot_count).reshape(bin_count, per_bin)
    count_out = place_tags(sample_count, placed, slot_count).reshape(bin_count, per_bin)
    spokes, segments, counts = (
        lax.all_to_all(spoke_out, "bin", split_axis=0, concat_axis=0, tiled=True),
        lax.all_to_all(segment_out, "bin", split_axis=0, concat_axis=0, tiled=True),
        lax.all_to_all(count_out, "bin", split_axis=0, concat_axis=0, tiled=True),
    )
    x_table = phase_table(
        jnp.arange(NXI, dtype=jnp.int32) - NXI // 2, jnp.arange(NG, dtype=jnp.int32) - NG // 2, NG
    )
    tile_data = arrived.reshape(bin_count, KP, CAPK, P_SIZE * 2 * C)
    spoke_sample_grid = spokes.reshape(bin_count, KP, CAPK)
    segment_grid = segments.reshape(bin_count, KP, CAPK)
    count_grid = counts.reshape(bin_count, KP, CAPK)
    kept = []
    for partition in range(KP):
        across_bins, weighted_values, columns = tile_lines(
            tile_data[:, partition].reshape(bin_count * CAPK, P_SIZE * 2 * C),
            spoke_sample_grid[:, partition].reshape(-1),
            segment_grid[:, partition].reshape(-1),
            count_grid[:, partition].reshape(-1),
            P_SIZE,
            RO,
            NG,
            R,
            WY,
            C,
        )
        tile_partial_sums = jnp.einsum(
            "sbm,sbg->smg", across_bins, weighted_values, preferred_element_type=jnp.float32
        )
        gridded = jax.ops.segment_sum(
            tile_partial_sums.reshape(-1, features), columns.reshape(-1), num_segments=NG
        ).astype(jnp.bfloat16)
        transformed = jnp.dot(x_table, gridded, preferred_element_type=jnp.float32).reshape(
            2, NXI, 2, C * WY
        )
        real_part = transformed[0, :, 0] - transformed[1, :, 1]
        imag_part = transformed[0, :, 1] + transformed[1, :, 0]
        spectrum = (
            jnp.stack([real_part, imag_part], axis=1).astype(jnp.bfloat16).reshape(NXI, features)
        )
        kept.append(spectrum)
    kz_depth = sensitivity.shape[0]
    columns_dev = NXI // slab_count
    slice_order = jnp.arange(kz_depth, dtype=jnp.int32)
    received = lax.all_to_all(
        jnp.stack(kept, axis=0), "slab", split_axis=1, concat_axis=0, tiled=True
    ).reshape(kz_depth, columns_dev * features)
    z_table = phase_table(slice_order - kz_depth // 2, slice_order - kz_depth // 2, kz_depth)
    transformed_z = jnp.dot(z_table, received, preferred_element_type=jnp.float32)
    scaling = 1.0 / math.sqrt(P_SIZE * bin_count * BLKB * kz_depth * C / KP)
    data_term = combine_coils(transformed_z, sensitivity, columns_dev, C, WY) * scaling
    current = image[0].reshape(kz_depth, columns_dev, 2, WY)
    weight = tv_weight[0].reshape(kz_depth, columns_dev, WY)
    is_last = my_bin == bin_count - 1
    above = from_behind(image, "bin", -1)[0].reshape(kz_depth, columns_dev, 2, WY)
    own_edge = jnp.where(is_last, 0.0, edge_flux(current, above, weight))
    below_edge = from_behind(own_edge.reshape(image.shape), "bin", 1)[0].reshape(
        kz_depth, columns_dev, 2, WY
    )
    gradient = below_edge - own_edge - data_term
    return gradient.reshape(image.shape)


def solution(mesh):
    return jax.shard_map(
        shards,
        mesh=mesh,
        in_specs=(
            P(("bin", "slab"), None),
            P(("bin", "slab"), None),
            P(("bin", "slab")),
            P(("bin", "slab")),
            P(("bin", "slab")),
            P(None, "slab"),
            P("bin", None, "slab"),
            P("bin", None, "slab"),
        ),
        out_specs=P("bin", None, "slab"),
        check_vma=False,
    )
```

profile of v0, /device:TPU:1, one launch (start us, length us, event | category | flops | bytes accessed | tf_op | source)
XLA Modules:
  0.0 299.7 jit_solution(12813548295601908873)
XLA Ops:
  3.8 11.5 %all-to-all-start.1 = ((s32[8,1,12]{2,1,0:T(1,128)}), s32[8,1,12]{2,1,0:T(1,128)S(1)}, u32[]{:S(2)}, u32[]{:S(2)}) async-start(s32[8,1,12]{2,1,0:T(1,128)} %bitcast.13), calls=%async_computation.1 | async-start | bytes 8192 | tf_op jit(solution)/shard_map/all_to_all | solution.py:149
  24.1 7.2 %all-to-all-start = ((s32[8,1,12]{2,1,0:T(1,128)}), s32[8,1,12]{2,1,0:T(1,128)S(1)}, u32[]{:S(2)}, u32[]{:S(2)}) async-start(s32[8,1,12]{2,1,0:T(1,128)} %bitcast.12), calls=%async_computation | async-start | bytes 8192 | tf_op jit(solution)/shard_map/all_to_all | solution.py:150
  31.7 8.5 %all-to-all-done = s32[8,1,12]{2,1,0:T(1,128)S(1)} async-done(((s32[8,1,12]{2,1,0:T(1,128)}), s32[8,1,12]{2,1,0:T(1,128)S(1)}, u32[]{:S(2)}, u32[]{:S(2)}) %all-to-all-start) | async-done | bytes 416 | tf_op jit(solution)/shard_map/all_to_all | solution.py:150
  40.2 3.3 %all-to-all-start.2 = ((s32[8,1,12]{2,1,0:T(1,128)}), s32[8,1,12]{2,1,0:T(1,128)S(1)}, u32[]{:S(2)}, u32[]{:S(2)}) async-start(s32[8,1,12]{2,1,0:T(1,128)} %bitcast.14), calls=%async_computation.2 | async-start | bytes 8192 | tf_op jit(solution)/shard_map/all_to_all | solution.py:151
  47.0 5.4 %all-to-all-done.2 = s32[8,1,12]{2,1,0:T(1,128)S(1)} async-done(((s32[8,1,12]{2,1,0:T(1,128)}), s32[8,1,12]{2,1,0:T(1,128)S(1)}, u32[]{:S(2)}, u32[]{:S(2)}) %all-to-all-start.2) | async-done | bytes 416 | tf_op jit(solution)/shard_map/all_to_all | solution.py:151
  52.4 3.9 %all-to-all-start.3 = ((bf16[8,12,2048]{2,1,0:T(8,128)(2,1)}), bf16[8,12,2048]{2,1,0:T(8,128)(2,1)S(1)}, u32[]{:S(2)}, u32[]{:S(2)}) async-start(bf16[8,12,2048]{2,1,0:T(8,128)(2,1)} %reshape.1120), calls=%async_computation.3 | async-start | bytes 1048576 | tf_op jit(solution)/shard_map/all_to_all | solution.py:138
  62.5 14.8 %multiply_reduce_fusion.5 = (f32[32,32,16]{1,2,0:T(8,128)S(1)}, f32[32,32,16]{1,2,0:T(8,128)S(1)}, f32[32,32,16]{1,2,0:T(8,128)}, f32[32,32,16]{1,2,0:T(8,128)},...) fusion(s32[32,32,4]{1,2,0:T(4,128)S(1)} %fusion.127, s32[16]{0:T(128)S(1)} %iota_add_fusion.8, ...), kind=kLoop, calls=%fused_computation.51 | loop fusion | flops 2457600 | bytes 491584 | tf_op jit(solution)/shard_map/reduce_sum | solution.py:76
  80.7 3.7 %subtract_convert_fusion.2 = (bf16[32,32,1,32,16]{1,4,3,2,0:T(8,128)(2,1)S(1)}, bf16[32,32,1,32,16]{1,4,3,2,0:T(8,128)(2,1)}) fusion(f32[32,32,32]{1,2,0:T(8,128)S(1)} %copy.208, f32[32,32,16]{1,2,0:T(8,128)S(1)} %get-tuple-element.8, f32[32,32,32]{1,2,0:T(8,128)S(1)} %copy.207, f32[32,32,16]{1,2,0:T(8,128)S(1)} %get-tuple-element.7), kind=kLoop, calls=%fused_computation.15 | loop fusion | flops 4194304 | bytes 2490368 | tf_op jit(solution)/shard_map/convert.20
  84.4 7.1 %pad_maximum_fusion = bf16[32,32,2,32,16]{1,4,3,2,0:T(8,128)(2,1)} fusion(bf16[32,32,1,32,16]{1,4,3,2,0:T(8,128)(2,1)} %get-tuple-element.38, bf16[32,32,1,32,16]{1,4,3,2,0:T(8,128)(2,1)S(1)} %get-tuple-element.37), kind=kLoop, calls=%fused_computation.7 | loop fusion | flops 1048576 | bytes 4194304 | tf_op jit(solution)/shard_map/stack | solution.py:83
  91.5 9.6 %fusion.75 = f32[32,40,1024]{2,1,0:T(8,128)} fusion(bf16[32,32,1024]{1,2,0:T(8,128)(2,1)} %bitcast.142, f32[32,32]{1,0:T(8,128)S(1)} %copy-done.12, f32[32,40]{1,0:T(8,128)S(1)} %copy-done.11, f32[32,32]{1,0:T(8,128)S(1)} %get-tuple-element.63), kind=kOutput, calls=%fused_computation.136 | convolution fusion | flops 84582400 | bytes 7353344 | tf_op jit(solution)/shard_map/sbm,sbg->smg/dot_general | solution.py:174
  101.1 15.5 %scatter_custom_fusion.4 = f32[384,1024]{1,0:T(8,128)S(1)} fusion(s32[1280]{0:T(1024)} %fusion.145, f32[1280,1024]{1,0:T(8,128)} %bitcast.150, f32[]{:T(128)} %constant.147.clone.1), kind=kCustom, calls=%fused_computation.74 | custom fusion | flops 1310720 | bytes 1573376 | tf_op jit(solution)/shard_map/scatter-add | solution.py:177
  131.9 9.5 %subtract_convert_fusion = (bf16[32,32,1,32,16]{1,4,3,2,0:T(8,128)(2,1)}, bf16[32,32,1,32,16]{1,4,3,2,0:T(8,128)(2,1)}, bf16[32,32,1,32,16]{1,4,3,2,0:T(8,128)(2,1)S(1)}, bf16[32,32,1,32,16]{1,4,3,2,0:T(8,128)(2,1)}) fusion(f32[32,32,32]{1,2,0:T(8,128)S(1)} %copy.232, f32[32,32,16]{1,2,0:T(8,128)} %get-tuple-element.15, f32[32,32,32]{1,2,0:T(8,128)S(1)} %copy.231, ...), kind=kLoop, calls=%fused_computation.11 | loop fusion | flops 8388608 | bytes 4980736 | tf_op jit(solution)/shard_map/convert.8
  141.5 7.1 %pad_maximum_fusion.1 = bf16[32,32,2,32,16]{1,4,3,2,0:T(8,128)(2,1)} fusion(bf16[32,32,1,32,16]{1,4,3,2,0:T(8,128)(2,1)S(1)} %get-tuple-element.80, bf16[32,32,1,32,16]{1,4,3,2,0:T(8,128)(2,1)} %get-tuple-element.81), kind=kLoop, calls=%fused_computation.8 | loop fusion | flops 1048576 | bytes 4194304 | tf_op jit(solution)/shard_map/stack | solution.py:83
  148.6 9.6 %fusion.73 = f32[32,40,1024]{2,1,0:T(8,128)} fusion(bf16[32,32,1024]{1,2,0:T(8,128)(2,1)} %bitcast.143, f32[32,32]{1,0:T(8,128)S(1)} %copy-done.10, f32[32,40]{1,0:T(8,128)S(1)} %copy-done.9, f32[32,32]{1,0:T(8,128)S(1)} %copy-done.6), kind=kOutput, calls=%fused_computation.135 | convolution fusion | flops 84582400 | bytes 7353344 | tf_op jit(solution)/shard_map/sbm,sbg->smg/dot_general | solution.py:174
  158.2 15.0 %scatter_custom_fusion.5 = f32[384,1024]{1,0:T(8,128)S(1)} fusion(s32[1280]{0:T(1024)} %fusion.146, f32[1280,1024]{1,0:T(8,128)} %bitcast.151, f32[]{:T(128)} %constant.147.clone.1), kind=kCustom, calls=%fused_computation.72 | custom fusion | flops 1310720 | bytes 1573376 | tf_op jit(solution)/shard_map/scatter-add | solution.py:177
  175.3 3.2 %reshape.1125 = f32[2,256,2,512]{3,2,1,0:T(2,128)S(1)} reshape(f32[512,1024]{1,0:T(8,128)} %fusion.23) | data formatting | bytes 4194304 | tf_op jit(solution)/shard_map/reshape | solution.py:180
  180.7 8.3 %pad_maximum_fusion.2 = bf16[32,32,2,32,16]{1,4,3,2,0:T(8,128)(2,1)} fusion(bf16[32,32,1,32,16]{1,4,3,2,0:T(8,128)(2,1)} %get-tuple-element.42, bf16[32,32,1,32,16]{1,4,3,2,0:T(8,128)(2,1)} %get-tuple-element.41), kind=kLoop, calls=%fused_computation.9 | loop fusion | flops 1048576 | bytes 4194304 | tf_op jit(solution)/shard_map/stack | solution.py:83
  189.0 9.6 %fusion.71 = f32[32,40,1024]{2,1,0:T(8,128)} fusion(bf16[32,32,1024]{1,2,0:T(8,128)(2,1)} %bitcast.144, f32[32,32]{1,0:T(8,128)S(1)} %copy-done.8, f32[32,40]{1,0:T(8,128)S(1)} %copy-done.7, f32[32,32]{1,0:T(8,128)S(1)} %get-tuple-element.67), kind=kOutput, calls=%fused_computation.134 | convolution fusion | flops 84582400 | bytes 7353344 | tf_op jit(solution)/shard_map/sbm,sbg->smg/dot_general | solution.py:174
  198.6 15.0 %scatter_custom_fusion.6 = f32[384,1024]{1,0:T(8,128)S(1)} fusion(s32[1280]{0:T(1024)} %fusion.147, f32[1280,1024]{1,0:T(8,128)} %bitcast.152, f32[]{:T(128)} %constant.147.clone.1), kind=kCustom, calls=%fused_computation.70 | custom fusion | flops 1310720 | bytes 1573376 | tf_op jit(solution)/shard_map/scatter-add | solution.py:177
  215.7 3.3 %reshape.1127 = f32[2,256,2,512]{3,2,1,0:T(2,128)S(1)} reshape(f32[512,1024]{1,0:T(8,128)} %fusion.21) | data formatting | bytes 4194304 | tf_op jit(solution)/shard_map/reshape | solution.py:180
  224.4 9.7 %all-to-all-start.4 = ((bf16[3,256,1024]{2,0,1:T(4,128)(2,1)}), bf16[3,256,1024]{2,0,1:T(4,128)(2,1)}, u32[]{:S(2)}, u32[]{:S(2)}) async-start(bf16[3,256,1024]{2,0,1:T(4,128)(2,1)} %copy.239), calls=%async_computation.4 | async-start | bytes 4194304 | tf_op jit(solution)/shard_map/all_to_all | solution.py:192
  241.6 4.2 %collective-permute-start.1 = (f32[1,96,256]{1,2,0:T(8,128)S(1)}, f32[1,96,256]{1,2,0:T(8,128)S(1)}, u32[]{:S(2)}, u32[]{:S(2)}) collective-permute-start(f32[1,96,256]{1,2,0:T(8,128)S(1)} %divide_select_fusion), channel_id=1, source_target_pairs={{0,32},{32,64},{64,96},{96,128},{128,160},{160,192},{192,224},{1,3... | collective-permute-start | bytes 294920 | tf_op jit(solution)/shard_map/ppermute | solution.py:28
  245.8 39.3 %all-to-all-done.4 = bf16[3,256,1024]{2,0,1:T(4,128)(2,1)} async-done(((bf16[3,256,1024]{2,0,1:T(4,128)(2,1)}), bf16[3,256,1024]{2,0,1:T(4,128)(2,1)}, u32[]{:S(2)}, u32[]{:S(2)}) %all-to-all-start.4) | async-done | bytes 1572896 | tf_op jit(solution)/shard_map/all_to_all | solution.py:192
  289.6 3.4 %copy.242 = bf16[8192,96]{1,0:T(8,128)(2,1)S(1)} copy(bf16[8192,96]{0,1:T(8,128)(2,1)} %bitcast.149) | data formatting | bytes 3145728 | tf_op jit(solution)/shard_map/dot_general | solution.py:196
  (167 shorter events, 70.8 us)
Async XLA Ops:
  3.8 20.3 %all-to-all-start.1 = ((s32[8,1,12]{2,1,0:T(1,128)}), s32[8,1,12]{2,1,0:T(1,128)S(1)}, u32[]{:S(2)}, u32[]{:S(2)}) async-start(s32[8,1,12]{2,1,0:T(1,128)} %bitcast.13), calls=%async_computation.1 | async-start | bytes 8192 | tf_op jit(solution)/shard_map/all_to_all | solution.py:149
  24.1 16.1 %all-to-all-start = ((s32[8,1,12]{2,1,0:T(1,128)}), s32[8,1,12]{2,1,0:T(1,128)S(1)}, u32[]{:S(2)}, u32[]{:S(2)}) async-start(s32[8,1,12]{2,1,0:T(1,128)} %bitcast.12), calls=%async_computation | async-start | bytes 8192 | tf_op jit(solution)/shard_map/all_to_all | solution.py:150
  40.2 12.2 %all-to-all-start.2 = ((s32[8,1,12]{2,1,0:T(1,128)}), s32[8,1,12]{2,1,0:T(1,128)S(1)}, u32[]{:S(2)}, u32[]{:S(2)}) async-start(s32[8,1,12]{2,1,0:T(1,128)} %bitcast.14), calls=%async_computation.2 | async-start | bytes 8192 | tf_op jit(solution)/shard_map/all_to_all | solution.py:151
  52.4 24.9 %all-to-all-start.3 = ((bf16[8,12,2048]{2,1,0:T(8,128)(2,1)}), bf16[8,12,2048]{2,1,0:T(8,128)(2,1)S(1)}, u32[]{:S(2)}, u32[]{:S(2)}) async-start(bf16[8,12,2048]{2,1,0:T(8,128)(2,1)} %reshape.1120), calls=%async_computation.3 | async-start | bytes 1048576 | tf_op jit(solution)/shard_map/all_to_all | solution.py:138
  84.4 7.1 %copy-start.11 = (f32[32,40]{1,0:T(8,128)S(1)}, f32[32,40]{1,0:T(8,128)}, u32[]{:S(2)}) copy-start(f32[32,40]{1,0:T(8,128)} %get-tuple-element.70) | copy-start | bytes 15364
  84.4 7.1 %copy-start.12 = (f32[32,32]{1,0:T(8,128)S(1)}, f32[32,32]{1,0:T(8,128)}, u32[]{:S(2)}) copy-start(f32[32,32]{1,0:T(8,128)} %fusion.142) | copy-start | bytes 12292
  121.7 3.0 %copy-start.4 = (f32[8,1,4,2048]{3,0,2,1:T(8,128)S(1)}, f32[8,1,4,2048]{3,0,2,1:T(8,128)}, u32[]{:S(2)}) copy-start(f32[8,1,4,2048]{3,0,2,1:T(8,128)} %get-tuple-element.51) | copy-start | bytes 786436
  123.6 3.8 %copy-start.3 = (f32[8,1,4,2048]{3,0,2,1:T(8,128)S(1)}, f32[8,1,4,2048]{3,0,2,1:T(8,128)}, u32[]{:S(2)}) copy-start(f32[8,1,4,2048]{3,0,2,1:T(8,128)} %get-tuple-element.50) | copy-start | bytes 786436
  141.5 7.1 %copy-start.6 = (f32[32,32]{1,0:T(8,128)S(1)}, f32[32,32]{1,0:T(8,128)}, u32[]{:S(2)}) copy-start(f32[32,32]{1,0:T(8,128)} %get-tuple-element.65) | copy-start | bytes 12292
  141.5 7.1 %copy-start.9 = (f32[32,40]{1,0:T(8,128)S(1)}, f32[32,40]{1,0:T(8,128)}, u32[]{:S(2)}) copy-start(f32[32,40]{1,0:T(8,128)} %get-tuple-element.73) | copy-start | bytes 15364
  141.5 7.1 %copy-start.10 = (f32[32,32]{1,0:T(8,128)S(1)}, f32[32,32]{1,0:T(8,128)}, u32[]{:S(2)}) copy-start(f32[32,32]{1,0:T(8,128)} %fusion.143) | copy-start | bytes 12292
  180.6 8.4 %copy-start.7 = (f32[32,40]{1,0:T(8,128)S(1)}, f32[32,40]{1,0:T(8,128)}, u32[]{:S(2)}) copy-start(f32[32,40]{1,0:T(8,128)} %get-tuple-element.76) | copy-start | bytes 15364
  180.6 8.3 %copy-start.8 = (f32[32,32]{1,0:T(8,128)S(1)}, f32[32,32]{1,0:T(8,128)}, u32[]{:S(2)}) copy-start(f32[32,32]{1,0:T(8,128)} %fusion.144) | copy-start | bytes 12292
  219.0 2.1 copy-start.2
  221.3 12.8 %copy-start.5 = (f32[1,96,256]{2,1,0:T(8,128)S(1)}, f32[1,96,256]{2,1,0:T(8,128)}, u32[]{:S(2)}) copy-start(f32[1,96,256]{2,1,0:T(8,128)} %param.14) | copy-start | bytes 294916
  224.4 14.2 %copy-start.13 = (f32[1,96,128]{2,1,0:T(8,128)S(1)}, f32[1,96,128]{2,1,0:T(8,128)}, u32[]{:S(2)}) copy-start(f32[1,96,128]{2,1,0:T(8,128)} %param.15) | copy-start | bytes 147460
  224.4 60.7 %all-to-all-start.4 = ((bf16[3,256,1024]{2,0,1:T(4,128)(2,1)}), bf16[3,256,1024]{2,0,1:T(4,128)(2,1)}, u32[]{:S(2)}, u32[]{:S(2)}) async-start(bf16[3,256,1024]{2,0,1:T(4,128)(2,1)} %copy.239), calls=%async_computation.4 | async-start | bytes 4194304 | tf_op jit(solution)/shard_map/all_to_all | solution.py:192
  234.2 7.2 %collective-permute-start = (f32[1,96,256]{1,2,0:T(8,128)S(1)}, f32[1,96,256]{1,2,0:T(8,128)S(1)}, u32[]{:S(2)}, u32[]{:S(2)}) collective-permute-start(f32[1,96,256]{1,2,0:T(8,128)S(1)} %copy.192), channel_id=1, source_target_pairs={{32,0},{64,32},{96,64},{128,96},{160,128},{192,160},{224,192},{33,... | collective-permute-start | bytes 294920 | tf_op jit(solution)/shard_map/ppermute | solution.py:28
  241.6 56.8 %collective-permute-start.1 = (f32[1,96,256]{1,2,0:T(8,128)S(1)}, f32[1,96,256]{1,2,0:T(8,128)S(1)}, u32[]{:S(2)}, u32[]{:S(2)}) collective-permute-start(f32[1,96,256]{1,2,0:T(8,128)S(1)} %divide_select_fusion), channel_id=1, source_target_pairs={{0,32},{32,64},{64,96},{96,128},{128,160},{160,192},{192,224},{1,3... | collective-permute-start | bytes 294920 | tf_op jit(solution)/shard_map/ppermute | solution.py:28
  292.9 1.6 copy-start
  293.0 2.2 copy-start.1
where the time goes:
time: 304 us; the launch traced here: 300 us
  other arithmetic  114 us (38%)
  waiting for transfers between devices  55 us (18%)
  local copies, waits for them, and re-layouts  52.5 us (17%)
  starting transfers between devices  41.1 us (14%)
  matrix products  36.3 us (12%)
    scatter-add x3, other arithmetic, shards(): jax.ops.segment_sum(tile_partial_sums.reshape(-1, features), columns.resh...  45.5 us
    all_to_all x1, waiting for transfers between devices, shards(): lax.all_to_all(jnp.stack(kept, axis=0), 'slab', split_axis=1, concat_axis...  39.3 us
    dot_general x3, matrix products, shards(): jnp.einsum('sbm,sbg->smg', across_bins, weighted_values, preferred_elemen...  28.8 us
    another operation x3, other arithmetic, tile_lines(): jnp.stack([real_part, imag_part], axis=2).astype(jnp.bfloat16)  22.5 us
    another operation x4, other arithmetic  15.3 us
    reduce_sum x1, other arithmetic, tile_lines(): real_weight = jnp.sum(tap_weight[:, :, :, None] * jnp.cos(angles), axis=2)  14.8 us
    all_to_all x1, starting transfers between devices, shards(): lax.all_to_all(spoke_out, 'bin', split_axis=0, concat_axis=0, tiled=True)  11.5 us
    all_to_all x1, starting transfers between devices, shards(): lax.all_to_all(jnp.stack(kept, axis=0), 'slab', split_axis=1, concat_axis...  9.67 us
  transfers between devices with their start and end apart: 7, of which 4 were waited for; matrix products, arithmetic and copies ran while one was open for 16% of the time, Pallas kernels for 0%

commit v1 on v0

v1 whole, which is shorter than its diff:
```python
import functools
import math

import jax
import jax.numpy as jnp
import ml_dtypes
import numpy as np
from jax import lax
from jax.experimental import pallas as pl
from jax.experimental.pallas import tpu as pltpu
from jax.sharding import PartitionSpec as P

C = 32
NG = 384
NXI = 256
WY = 16
RO = 384
P_SIZE = 32
KP = 3
BLKB = 4
CAPK = 4

SMOOTHING = 0.5
GOLDEN_STEP = 40503
TURN_STEPS = 65536

F32 = jnp.float32
BF16 = jnp.bfloat16
LANES = 128
PC = 2 * C
ROUTE_ROWS = KP * PC
COIL_GROUPS = 4
GC = C // COIL_GROUPS
MESH = pl.DeviceIdType.MESH
FAR = -1000.0


def iota(shape, dim):
    return lax.broadcasted_iota(jnp.int32, shape, dim)


def turn_waves(turns):
    quarter = jnp.floor(4.0 * turns + 0.5)
    angle = (2.0 * math.pi) * (turns - 0.25 * quarter)
    sq = angle * angle
    sine = angle + angle * sq * (
        -1.0 / 6 + sq * (1.0 / 120 + sq * (-1.0 / 5040 + sq * (1.0 / 362880)))
    )
    cosine = 1.0 + sq * (
        -0.5 + sq * (1.0 / 24 + sq * (-1.0 / 720 + sq * (1.0 / 40320 + sq * (-1.0 / 3628800))))
    )
    turn = quarter - 4.0 * jnp.floor(0.25 * quarter)
    odd = (turn == 1.0) | (turn == 3.0)
    first = jnp.where(odd, sine, cosine)
    second = jnp.where(odd, cosine, sine)
    cos_out = jnp.where((turn == 1.0) | (turn == 2.0), -first, first)
    sin_out = jnp.where(turn >= 2.0, -second, second)
    return cos_out, sin_out


def spline_weight(offset):
    distance = jnp.abs(offset)
    inside = 2.0 / 3.0 + distance * distance * (0.5 * distance - 1.0)
    rest = jnp.maximum(2.0 - distance, 0.0)
    return jnp.where(distance < 1.0, inside, rest * rest * (rest * (1.0 / 6.0)))


def all_bytes(ref, sem):
    pltpu.make_async_copy(ref, ref, sem).wait()


def route_kernel(
    bins,
    data_ref,
    route_ref,
    spoke_ref,
    segment_ref,
    count_ref,
    image_ref,
    weight_ref,
    tiles_out,
    coords_out,
    above_out,
    below_out,
    below_weight_out,
    stacked,
    placed_rows,
    tiles,
    coords,
    local_sems,
    send_sems,
    recv_sems,
):
    me = lax.axis_index("bin")
    barrier = pltpu.get_barrier_semaphore()
    for step in range(1, bins):
        pl.semaphore_signal(
            barrier, inc=1, device_id={"bin": lax.rem(me + step, bins)}, device_id_type=MESH
        )

    blocks = data_ref.shape[0]
    row = iota((blocks, LANES), 0)
    lane = iota((blocks, LANES), 1)
    lane_block = lane & (blocks - 1)
    route_col = jnp.broadcast_to(route_ref[...].astype(F32), (blocks, LANES))
    route_row = jnp.sum(jnp.where(row == lane_block, route_col, 0.0), axis=0, keepdims=True)
    same = route_col == jnp.broadcast_to(route_row, (blocks, LANES))
    rank_row = jnp.sum(jnp.where(same & (row < lane_block), 1.0, 0.0), axis=0, keepdims=True)
    rank_col = jnp.sum(jnp.where(same & (lane < row), 1.0, 0.0), axis=1, keepdims=True)
    slot_row = route_row * CAPK + rank_row

    def column(ref_row):
        spread = jnp.broadcast_to(ref_row.astype(F32), (blocks, blocks))
        eye = iota((blocks, blocks), 0) == iota((blocks, blocks), 1)
        return jnp.sum(jnp.where(eye, spread, 0.0), axis=1, keepdims=True)

    turn_row = (spoke_ref[...] * GOLDEN_STEP) & (TURN_STEPS - 1)
    columns = [
        column(turn_row >> 8),
        column(turn_row & 255),
        column(segment_ref[...]),
        column(count_ref[...]),
    ]
    slot_hit = rank_col == (lane & (CAPK - 1)).astype(F32)
    picks = [jnp.where(slot_hit, value, 0.0) for value in columns]
    picks = jnp.concatenate(picks, axis=1).astype(BF16)
    picks = jnp.concatenate(
        [picks, jnp.zeros((LANES - blocks, len(columns) * LANES), BF16)], axis=0
    )
    rows = 8 * bins
    out_row = iota((rows, LANES), 0)
    out_lane = iota((rows, LANES), 1)
    part = out_row & 7
    is_x = part < KP
    partition = jnp.where(is_x, part, part - KP)
    row_route = jnp.where(part < 2 * KP, KP * (out_row >> 3) + partition, -1).astype(F32)
    chosen = (row_route == jnp.broadcast_to(route_row, (rows, LANES))) & (out_lane < blocks)
    spread = jnp.dot(
        jnp.where(chosen, 1.0, 0.0).astype(BF16), picks, preferred_element_type=F32
    )
    turns = (256.0 * spread[:, :LANES] + spread[:, LANES : 2 * LANES]) * (1.0 / TURN_STEPS)
    segment = spread[:, 2 * LANES : 3 * LANES]
    count = spread[:, 3 * LANES :]
    cosine, sine = turn_waves(turns)
    sample = (2 * ((out_lane & 63) >> 2) + (out_lane >> 6)).astype(F32)
    radial = (P_SIZE * segment + sample - RO // 2 + 0.5) * ((NG - 8) / RO)
    coord_x = jnp.where(sample < count, NG / 2 + radial * cosine, FAR)
    coord_y = NG / 2 + radial * sine
    coords[...] = jnp.where(is_x, coord_x, coord_y)

    big = (bins * KP * 16, LANES)
    place_row = iota(big, 0)
    place_lane = iota(big, 1)
    wanted = (CAPK * (place_row >> 4) + (place_row & 3)).astype(F32)
    hit = (wanted == jnp.broadcast_to(slot_row, big)) & (((place_row >> 2) & 3) == (place_lane >> 5))
    place = jnp.where(hit, 1.0, 0.0).astype(BF16)
    for quarter in range(4):
        for fourth in range(4):
            first = (4 * fourth + quarter) * LANES
            stacked[quarter * blocks : (quarter + 1) * blocks, fourth * LANES : (fourth + 1) * LANES] = (
                data_ref[:, first : first + LANES]
            )
    placed_rows[...] = jnp.dot(place, stacked[...], preferred_element_type=F32)

    half_lane = iota((PC, LANES), 1) < 64

    def turn_pair(pair, carry):
        base = pl.multiple_of(pair * 32, 32)
        pieces = [
            placed_rows[pl.ds(base + 16 * route, 16), fourth * LANES : (fourth + 1) * LANES]
            for route in range(2)
            for fourth in range(4)
        ]
        turned = jnp.concatenate(pieces, axis=0).T
        low, high = turned[:PC], turned[PC:]
        first = jnp.where(half_lane, low, pltpu.roll(high, 64, 1))
        second = jnp.where(half_lane, pltpu.roll(low, 64, 1), high)
        at = pl.multiple_of(pair * 2 * PC, 2 * PC)
        tiles[pl.ds(at, PC), :] = first.astype(BF16)
        tiles[pl.ds(at + PC, PC), :] = second.astype(BF16)
        return carry

    lax.fori_loop(0, bins * KP // 2, turn_pair, 0)

    pl.semaphore_wait(barrier, bins - 1)

    def tile_rows(index):
        return pl.ds(pl.multiple_of(index * ROUTE_ROWS, ROUTE_ROWS), ROUTE_ROWS)

    def coord_rows(index):
        return pl.ds(pl.multiple_of(index * 8, 8), 8)

    up = {"bin": lax.rem(me + 1, bins)}
    down = {"bin": lax.rem(me + bins - 1, bins)}
    edge_copies = [
        pltpu.make_async_remote_copy(
            image_ref, above_out, send_sems.at[2], recv_sems.at[2], down, MESH
        ),
        pltpu.make_async_remote_copy(
            image_ref, below_out, send_sems.at[3], recv_sems.at[3], up, MESH
        ),
        pltpu.make_async_remote_copy(
            weight_ref, below_weight_out, send_sems.at[4], recv_sems.at[4], up, MESH
        ),
    ]
    for step in range(1, bins):
        peer = lax.rem(me + step, bins)
        pltpu.make_async_remote_copy(
            coords.at[coord_rows(peer)],
            coords_out.at[coord_rows(me)],
            send_sems.at[0],
            recv_sems.at[0],
            {"bin": peer},
            MESH,
        ).start()
        pltpu.make_async_remote_copy(
            tiles.at[tile_rows(peer)],
            tiles_out.at[tile_rows(me)],
            send_sems.at[1],
            recv_sems.at[1],
            {"bin": peer},
            MESH,
        ).start()
    for copy in edge_copies:
        copy.start()
    own = [
        pltpu.make_async_copy(
            coords.at[coord_rows(me)], coords_out.at[coord_rows(me)], local_sems.at[0]
        ),
        pltpu.make_async_copy(
            tiles.at[tile_rows(me)], tiles_out.at[tile_rows(me)], local_sems.at[1]
        ),
    ]
    for copy in own:
        copy.start()
    for copy in own:
        copy.wait()
    others = pl.ds(0, (bins - 1) * 8)
    all_bytes(coords_out.at[others], recv_sems.at[0])
    all_bytes(coords.at[others], send_sems.at[0])
    others = pl.ds(0, (bins - 1) * ROUTE_ROWS)
    all_bytes(tiles_out.at[others], recv_sems.at[1])
    all_bytes(tiles.at[others], send_sems.at[1])
    for copy in edge_copies:
        copy.wait()


def route_samples(bins, data, routes, spokes, segments, counts, image, weight):
    any_space = pl.BlockSpec(memory_space=pl.ANY)
    vmem = pl.BlockSpec(memory_space=pltpu.VMEM)
    blocks = data.shape[0]
    route_count = bins * KP
    return pl.pallas_call(
        functools.partial(route_kernel, bins),
        out_shape=(
            jax.ShapeDtypeStruct((bins * ROUTE_ROWS, LANES), BF16),
            jax.ShapeDtypeStruct((bins * 8, LANES), F32),
            jax.ShapeDtypeStruct(image.shape, F32),
            jax.ShapeDtypeStruct(image.shape, F32),
            jax.ShapeDtypeStruct(weight.shape, F32),
        ),
        in_specs=[vmem] * 5 + [any_space] * 2,
        out_specs=(any_space,) * 5,
        scratch_shapes=[
            pltpu.VMEM((4 * blocks, 4 * LANES), BF16),
            pltpu.VMEM((route_count * 16, 4 * LANES), F32),
            pltpu.VMEM((bins * ROUTE_ROWS, LANES), BF16),
            pltpu.VMEM((bins * 8, LANES), F32),
            pltpu.SemaphoreType.DMA((2,)),
            pltpu.SemaphoreType.DMA((5,)),
            pltpu.SemaphoreType.DMA((5,)),
        ],
        compiler_params=pltpu.CompilerParams(
            collective_id=0, has_side_effects=True, vmem_limit_bytes=32 << 20
        ),
    )(data, routes, spokes, segments, counts, image, weight)


def grid_kernel(
    bins,
    slabs,
    tiles_ref,
    coords_ref,
    x_table_ref,
    z_table_ref,
    sens_hbm,
    image_ref,
    above_ref,
    below_ref,
    weight_ref,
    below_weight_ref,
    out_ref,
    samples,
    row_real,
    row_imag,
    across,
    weighted,
    sending,
    received,
    sens,
    widened,
    total,
    local_sems,
    send_sems,
    recv_sems,
):
    me = lax.axis_index("slab")
    my_bin = lax.axis_index("bin")
    barrier = pltpu.get_barrier_semaphore()

    def greet(step, carry):
        pl.semaphore_signal(
            barrier, inc=1, device_id={"slab": lax.rem(me + step, slabs)}, device_id_type=MESH
        )
        return carry

    lax.fori_loop(1, slabs, greet, 0)
    sens_copy = pltpu.make_async_copy(sens_hbm, sens, local_sems.at[0])
    sens_copy.start()

    y_offset = (iota((WY, LANES), 0) - WY // 2).astype(F32)
    taps = [turn_waves(y_offset * (m / NG)) for m in range(1, 4)]

    def prepare(step, carry):
        source = lax.rem(step, bins)
        part = lax.div(step, bins)
        rows = pl.ds(pl.multiple_of(part * PC, PC), PC)
        samples[source, rows, :] = tiles_ref[source, rows, :].astype(F32)
        coord_x = coords_ref[source, pl.ds(part, 1), :]
        coord_y = coords_ref[source, pl.ds(KP + part, 1), :]
        cell = jnp.floor(coord_y)
        ahead = coord_y - cell
        behind = 1.0 - ahead
        weights = [
            behind * behind * behind * (1.0 / 6.0),
            2.0 / 3.0 + ahead * ahead * (0.5 * ahead - 1.0),
            2.0 / 3.0 + behind * behind * (0.5 * behind - 1.0),
            ahead * ahead * ahead * (1.0 / 6.0),
        ]
        steps = y_offset * (cell - (1.0 + NG // 2))
        turns = steps * (1.0 / NG)
        base_cos, base_sin = turn_waves(turns - jnp.floor(turns))
        sum_cos = jnp.broadcast_to(weights[0], (WY, LANES))
        sum_sin = jnp.zeros((WY, LANES), F32)
        for weight, (tap_cos, tap_sin) in zip(weights[1:], taps):
            sum_cos = sum_cos + weight * tap_cos
            sum_sin = sum_sin + weight * tap_sin
        at = pl.ds(pl.multiple_of(step * WY, WY), WY)
        row_real[at, :] = sum_cos * base_cos - sum_sin * base_sin
        row_imag[at, :] = sum_cos * base_sin + sum_sin * base_cos
        lanes = pl.ds(pl.multiple_of(source * LANES, LANES), LANES)
        piece = 32
        for first in range(0, NG, piece):
            column = (iota((piece, LANES), 0) + first).astype(F32)
            across[part, first : first + piece, lanes] = spline_weight(coord_x - column).astype(BF16)
        return carry

    lax.fori_loop(0, KP * bins, prepare, 0)

    def slab_copy(group, step):
        peer = lax.rem(me + step, slabs)
        return pltpu.make_async_remote_copy(
            sending.at[group, peer],
            received.at[group, me],
            send_sems.at[group],
            recv_sems.at[group],
            {"slab": peer},
            MESH,
        )

    def own_copy(group):
        return pltpu.make_async_copy(
            sending.at[group, me], received.at[group, me], local_sems.at[1 + group]
        )

    for group in range(COIL_GROUPS):

        def grid_part(part, carry, group=group):
            def weigh(source, carry):
                at = pl.ds(pl.multiple_of((part * bins + source) * WY, WY), WY)
                real, imag = row_real[at, :], row_imag[at, :]
                lanes = pl.ds(pl.multiple_of(source * LANES, LANES), LANES)
                for coil in range(GC):
                    row = part * PC + group * GC + coil
                    data_real = samples[source, pl.ds(row, 1), :]
                    data_imag = samples[source, pl.ds(row + C, 1), :]
                    weighted[coil * WY : (coil + 1) * WY, lanes] = (
                        real * data_real - imag * data_imag
                    ).astype(BF16)
                    weighted[(GC + coil) * WY : (GC + coil + 1) * WY, lanes] = (
                        real * data_imag + imag * data_real
                    ).astype(BF16)
                return carry

            lax.fori_loop(0, bins, weigh, 0)
            lines = lax.dot_general(
                across[part],
                weighted[...],
                (((1,), (1,)), ((), ())),
                preferred_element_type=F32,
            ).astype(BF16)
            stacked = jnp.concatenate([lines[:, :LANES], lines[:, LANES:]], axis=0)
            spectra = jnp.dot(x_table_ref[...], stacked, preferred_element_type=F32)
            rows = 2 * NXI // slabs
            at = pl.ds(pl.multiple_of(part * rows, rows), rows)
            sending[group, :, at, :] = spectra.astype(BF16).reshape(slabs, rows, LANES)
            return carry

        lax.fori_loop(0, KP, grid_part, 0)
        if group == 0:
            pl.semaphore_wait(barrier, slabs - 1)

        def send(step, carry, group=group):
            slab_copy(group, step).start()
            return carry

        lax.fori_loop(1, slabs, send, 0)
        own_copy(group).start()

    sens_copy.wait()
    depth = KP * slabs
    rows = 2 * NXI // slabs
    features = GC * WY
    for group in range(COIL_GROUPS):
        own_copy(group).wait()
        others = pl.ds(0, slabs - 1)
        all_bytes(received.at[group, others], recv_sems.at[group])

        def widen(source, carry, group=group):
            at = pl.ds(source * KP, KP)
            widened[at] = received[group, source].astype(F32).reshape(KP, rows, LANES)
            return carry

        lax.fori_loop(0, slabs, widen, 0)
        for pair in range(rows // 4):
            columns = []
            for column in (2 * pair, 2 * pair + 1):
                real = widened[:, 2 * column, :].astype(BF16)
                imag = widened[:, 2 * column + 1, :].astype(BF16)
                columns.append(jnp.concatenate([real, imag], axis=0))
            images = jnp.dot(
                z_table_ref[...],
                jnp.concatenate(columns, axis=1),
                preferred_element_type=F32,
            )
            for at, column in enumerate((2 * pair, 2 * pair + 1)):
                image_real = images[:depth, at * LANES : (at + 1) * LANES]
                image_imag = images[depth:, at * LANES : (at + 1) * LANES]
                first = 2 * column * C * WY + group * features
                sens_real = sens[:, first : first + features].astype(F32)
                first = first + C * WY
                sens_imag = sens[:, first : first + features].astype(F32)
                real = sens_real * image_real + sens_imag * image_imag
                imag = sens_real * image_imag - sens_imag * image_real
                if group > 0:
                    real = real + total[2 * column]
                    imag = imag + total[2 * column + 1]
                total[2 * column] = real
                total[2 * column + 1] = imag

    for group in range(COIL_GROUPS):
        all_bytes(sending.at[group, pl.ds(0, slabs - 1)], send_sems.at[group])

    scaling = 1.0 / math.sqrt(P_SIZE * bins * BLKB * depth * C / KP)
    data_term = []
    place = iota((depth, LANES), 1) >> 4
    for half in range(rows // 8):
        line = jnp.zeros((depth, LANES), F32)
        for at in range(8):
            value = total[half * 8 + at]
            for shift in (64, 32, 16):
                value = value + pltpu.roll(value, shift, 1)
            line = jnp.where(place == at, value, line)
        data_term.append(line * scaling)
    data_term = jnp.concatenate(data_term, axis=1)

    wide = out_ref.shape[1]
    lane = iota((depth, wide), 1)
    upper_half = ((lane >> 4) & 1) == 1
    from_lane = iota((wide // 2, wide), 0)
    to_lane = iota((wide // 2, wide), 1)
    widen_weight = jnp.where(
        from_lane == ((to_lane >> 5) << 4) + (to_lane & 15), 1.0, 0.0
    )

    def edge(difference, weight):
        square = difference * difference
        other = jnp.where(
            upper_half, pltpu.roll(square, 16, 1), pltpu.roll(square, wide - 16, 1)
        )
        magnitude = jnp.sqrt(square + other + SMOOTHING * SMOOTHING)
        spread = jnp.dot(
            weight, widen_weight, preferred_element_type=F32, precision=lax.Precision.HIGHEST
        )
        return spread * difference / magnitude

    current = image_ref[...]
    own_edge = edge(above_ref[...] - current, weight_ref[...])
    below_edge = edge(current - below_ref[...], below_weight_ref[...])
    own_edge = jnp.where(my_bin == bins - 1, 0.0, own_edge)
    below_edge = jnp.where(my_bin == 0, 0.0, below_edge)
    out_ref[...] = below_edge - own_edge - data_term


def grid_and_combine(
    bins, slabs, tiles, coords, x_table, z_table, sens, image, above, below, weight, below_weight
):
    any_space = pl.BlockSpec(memory_space=pl.ANY)
    vmem = pl.BlockSpec(memory_space=pltpu.VMEM)
    depth = sens.shape[0]
    rows = 2 * NXI // slabs
    return pl.pallas_call(
        functools.partial(grid_kernel, bins, slabs),
        out_shape=jax.ShapeDtypeStruct(image.shape, F32),
        in_specs=[vmem] * 4 + [any_space] + [vmem] * 5,
        out_specs=vmem,
        scratch_shapes=[
            pltpu.VMEM((bins, ROUTE_ROWS, LANES), F32),
            pltpu.VMEM((KP * bins * WY, LANES), F32),
            pltpu.VMEM((KP * bins * WY, LANES), F32),
            pltpu.VMEM((KP, NG, bins * LANES), BF16),
            pltpu.VMEM((2 * GC * WY, bins * LANES), BF16),
            pltpu.VMEM((COIL_GROUPS, slabs, KP * rows, LANES), BF16),
            pltpu.VMEM((COIL_GROUPS, slabs, KP * rows, LANES), BF16),
            pltpu.VMEM(sens.shape, BF16),
            pltpu.VMEM((depth, rows, LANES), F32),
            pltpu.VMEM((rows, depth, LANES), F32),
            pltpu.SemaphoreType.DMA((1 + COIL_GROUPS,)),
            pltpu.SemaphoreType.DMA((COIL_GROUPS,)),
            pltpu.SemaphoreType.DMA((COIL_GROUPS,)),
        ],
        compiler_params=pltpu.CompilerParams(
            collective_id=1, has_side_effects=True, vmem_limit_bytes=48 << 20
        ),
    )(tiles, coords, x_table, z_table, sens, image, above, below, weight, below_weight)


def x_phases():
    out_index = np.arange(NXI) - NXI // 2
    in_index = np.arange(NG) - NG // 2
    angles = 2.0 * math.pi / NG * (out_index[:, None] * in_index[None, :] % NG)
    cosine, sine = np.cos(angles), np.sin(angles)
    table = np.stack(
        [np.concatenate([cosine, -sine], axis=1), np.concatenate([sine, cosine], axis=1)], axis=1
    )
    return table.reshape(2 * NXI, 2 * NG)


def z_phases(depth):
    index = np.arange(depth) - depth // 2
    angles = 2.0 * math.pi / depth * (index[:, None] * index[None, :] % depth)
    cosine, sine = np.cos(angles), np.sin(angles)
    return np.concatenate(
        [np.concatenate([cosine, -sine], axis=1), np.concatenate([sine, cosine], axis=1)], axis=0
    )


def shards(
    sample_data,
    block_route,
    spoke_index,
    segment_index,
    sample_count,
    sensitivity,
    image,
    tv_weight,
):
    bins = lax.axis_size("bin")
    slabs = lax.axis_size("slab")
    x_table = jnp.asarray(x_phases().astype(ml_dtypes.bfloat16))
    z_table = jnp.asarray(z_phases(sensitivity.shape[0]).astype(ml_dtypes.bfloat16))
    current = image[0]
    weight = tv_weight[0]
    tiles, coords, above, below, below_weight = route_samples(
        bins,
        sample_data,
        block_route,
        spoke_index.reshape(1, -1),
        segment_index.reshape(1, -1),
        sample_count.reshape(1, -1),
        current,
        weight,
    )
    gradient = grid_and_combine(
        bins,
        slabs,
        tiles.reshape(bins, ROUTE_ROWS, LANES),
        coords.reshape(bins, 8, LANES),
        x_table,
        z_table,
        sensitivity,
        current,
        above,
        below,
        weight,
        below_weight,
    )
    return gradient.reshape(image.shape)


def solution(mesh):
    return jax.shard_map(
        shards,
        mesh=mesh,
        in_specs=(
            P(("bin", "slab"), None),
            P(("bin", "slab"), None),
            P(("bin", "slab")),
            P(("bin", "slab")),
            P(("bin", "slab")),
            P(None, "slab"),
            P("bin", None, "slab"),
            P("bin", None, "slab"),
        ),
        out_specs=P("bin", None, "slab"),
        check_vma=False,
    )
```

time: 304 us -> 84.1 us (0.28); the launches traced: 300 us -> 83.4 us
  other arithmetic: 114 us -> 0 us
  Pallas kernels: 0 us -> 72.3 us
  waiting for transfers between devices: 55 us -> 0 us
  local copies, waits for them, and re-layouts: 52.5 us -> 11.1 us
  starting transfers between devices: 41.1 us -> 0 us
  matrix products: 36.3 us -> 0 us
    pallas_call x0 -> x2, Pallas kernels: none -> 72.3 us  [the longest x1 47.6 us: grid_and_combine(): pl.pallas_call(functools.partial(grid_kernel, bins, slabs), out_shape=jax...]
    all_to_all x5 -> x0, waiting for transfers between devices: 55 us -> none  [the longest x1 39.3 us: shards(): lax.all_to_all(jnp.stack(kept, axis=0), 'slab', split_axis=1, concat_axis...]
    scatter-add x3 -> x0, other arithmetic: 45.5 us -> none  [shards(): jax.ops.segment_sum(tile_partial_sums.reshape(-1, features), columns.resh...]
    another operation x12 -> x0, other arithmetic: 38.2 us -> none  [the longest x3 22.5 us: tile_lines(): jnp.stack([real_part, imag_part], axis=2).astype(jnp.bfloat16)]
    dot_general x7 -> x0, matrix products: 36.3 us -> none  [the longest x3 28.8 us: shards(): jnp.einsum('sbm,sbg->smg', across_bins, weighted_values, preferred_elemen...]
    all_to_all x5 -> x0, starting transfers between devices: 35.6 us -> none  [the longest x1 11.5 us: shards(): lax.all_to_all(spoke_out, 'bin', split_axis=0, concat_axis=0, tiled=True)]
    reduce_sum x4 -> x0, other arithmetic: 18.9 us -> none  [the longest x1 14.8 us: tile_lines(): real_weight = jnp.sum(tap_weight[:, :, :, None] * jnp.cos(angles), axis=2)]
    slice x11 -> x0, local copies, waits for them, and re-layouts: 11.4 us -> none  [the longest x3 4.86 us: shards(): real_part = transformed[0, :, 0] - transformed[1, :, 1]]
  transfers between devices with their start and end apart: 7 -> 0, of which waited for: 4 -> 0; matrix products, arithmetic and copies ran while one was open for 16% -> 0% of each run, Pallas kernels for 0% -> 0%
where the time goes in v1:
time: 84.1 us; the launch traced here: 83.4 us
  Pallas kernels  72.3 us (86%)
  local copies, waits for them, and re-layouts  11.1 us (13%)
    pallas_call x1, Pallas kernels, grid_and_combine(): pl.pallas_call(functools.partial(grid_kernel, bins, slabs), out_shape=jax...  47.6 us
    pallas_call x1, Pallas kernels, route_samples(): pl.pallas_call(functools.partial(route_kernel, bins), out_shape=(jax.Shap...  24.7 us
    unnamed x24, local copies, waits for them, and re-layouts  11.1 us

profile of v1, /device:TPU:1, one launch (start us, length us, event | category | flops | bytes accessed | tf_op | source)
XLA Modules:
  0.0 83.4 jit_solution(8082079263399377317)
XLA Ops:
  0.0 0.7 copy.11.route_ref
  0.7 0.0 copy-start.2
  0.7 0.9 %copy-done.2 = f32[1,96,256]{2,1,0:T(8,128)S(1)} copy-done((f32[1,96,256]{2,1,0:T(8,128)S(1)}, f32[1,96,256]{2,1,0:T(8,128)}, u32[]{:S(2)}) %copy-start.2) | copy-done | bytes 98328
  1.6 0.0 copy-start.4
  1.6 0.8 copy-done.4
  2.4 0.0 copy-start.6
  2.4 0.9 %copy-done.6 = bf16[32,2048]{1,0:T(8,128)(2,1)S(1)} copy-done((bf16[32,2048]{1,0:T(8,128)(2,1)S(1)}, bf16[32,2048]{1,0:T(8,128)(2,1)}, u32[]{:S(2)}) %copy-start.6) | copy-done | bytes 131096
  3.3 0.0 copy-start.8
  3.3 0.7 copy-done.8
  4.0 0.0 copy-start.9
  4.0 0.7 copy-done.9
  4.6 0.0 copy-start.10
  4.6 0.7 copy-done.10
  5.3 24.7 %shard_map.100 = (bf16[1536,128]{1,0:T(8,128)(2,1)S(1)}, f32[64,128]{1,0:T(8,128)S(1)}, f32[96,256]{1,0:T(8,128)S(1)}, f32[96,256]{1,0:T(8,128)S(1)}, f32[96,128]{1,0:T(8,128)S(1)}) custom-call(bf16[32,2048]{1,0:T(8,128)(2,1)S(1)} %copy-done.6, s32[32,1]{1,0:T(8,128)S(1)} %copy.11.route_ref, s32[1,32]{1,0:T(1,128)S(1)} %bitcast.15, s32[1,32]{1,0:T(1,128)S(1)} %bitcast.16, ...), custom_call_target="tpu_custom_call" | custom-call | tf_op jit(solution)/shard_map/pallas_call | solution.py:253
  30.0 0.0 copy-start
  30.1 1.4 %copy-done = bf16[96,8192]{1,0:T(8,128)(2,1)S(1)} copy-done((bf16[96,8192]{1,0:T(8,128)(2,1)S(1)}, bf16[96,8192]{1,0:T(8,128)(2,1)}, u32[]{:S(2)}) %copy-start) | copy-done | bytes 1572888
  31.5 0.0 copy-start.1
  31.5 1.1 %copy-done.1 = bf16[512,768]{1,0:T(8,128)(2,1)S(1)} copy-done((bf16[512,768]{1,0:T(8,128)(2,1)S(1)}, bf16[512,768]{1,0:T(8,128)(2,1)}, u32[]{:S(2)}) %copy-start.1) | copy-done | bytes 786456
  32.6 0.0 copy-start.3
  32.6 0.9 %copy-done.3 = f32[1,96,256]{2,1,0:T(8,128)S(1)} copy-done((f32[1,96,256]{2,1,0:T(8,128)S(1)}, f32[1,96,256]{2,1,0:T(8,128)}, u32[]{:S(2)}) %copy-start.3) | copy-done | bytes 98328
  33.5 0.8 copy-done.5
  34.3 0.9 %copy-done.7 = bf16[192,192]{1,0:T(8,128)(2,1)S(1)} copy-done((bf16[192,192]{1,0:T(8,128)(2,1)S(1)}, bf16[192,192]{1,0:T(8,128)(2,1)}, u32[]{:S(2)}) %copy-start.7) | copy-done | bytes 73752
  35.2 47.6 %shard_map.101 = f32[96,256]{1,0:T(8,128)S(1)} custom-call(bf16[8,192,128]{2,1,0:T(8,128)(2,1)S(1)} %bitcast.11, f32[8,8,128]{2,1,0:T(8,128)S(1)} %bitcast.14, bf16[512,768]{1,0:T(8,128)(2,1)S(1)} %copy-done.1, bf16[192,192]{1,0:T(8,128)(2,1)S(1)} %copy-done.7, bf16[96,8192]{1,0:T(8,128)(2,1)S(1)} %copy-done, f32[96,256]{1,0:T(8,128)S(1)} %bitcast.10, ...), custom_call_target="tpu_custom_call" | custom-call | tf_op jit(solution)/shard_map/pallas_call | solution.py:512
  82.8 0.6 copy.13
  (2 shorter events, 0.0 us)
Async XLA Ops:
  0.7 0.9 %copy-start.2 = (f32[1,96,256]{2,1,0:T(8,128)S(1)}, f32[1,96,256]{2,1,0:T(8,128)}, u32[]{:S(2)}) copy-start(f32[1,96,256]{2,1,0:T(8,128)} %param.16) | copy-start | bytes 294916
  1.6 0.8 copy-start.4
  2.4 0.9 %copy-start.6 = (bf16[32,2048]{1,0:T(8,128)(2,1)S(1)}, bf16[32,2048]{1,0:T(8,128)(2,1)}, u32[]{:S(2)}) copy-start(bf16[32,2048]{1,0:T(8,128)(2,1)} %data_ref.1) | copy-start | bytes 393220
  3.3 0.7 copy-start.8
  4.0 0.7 copy-start.9
  4.6 0.7 copy-start.10
  30.0 1.4 %copy-start = (bf16[96,8192]{1,0:T(8,128)(2,1)S(1)}, bf16[96,8192]{1,0:T(8,128)(2,1)}, u32[]{:S(2)}) copy-start(bf16[96,8192]{1,0:T(8,128)(2,1)} %sens_hbm.1) | copy-start | bytes 4718596
  31.5 1.1 %copy-start.1 = (bf16[512,768]{1,0:T(8,128)(2,1)S(1)}, bf16[512,768]{1,0:T(8,128)(2,1)}, u32[]{:S(2)}) copy-start(bf16[512,768]{1,0:T(8,128)(2,1)} %constant.4.clone.x_table_ref) | copy-start | bytes 2359300
  32.6 0.9 %copy-start.3 = (f32[1,96,256]{2,1,0:T(8,128)S(1)}, f32[1,96,256]{2,1,0:T(8,128)}, u32[]{:S(2)}) copy-start(f32[1,96,256]{2,1,0:T(8,128)} %param.16) | copy-start | bytes 294916
  33.5 0.8 copy-start.5
  34.3 0.9 %copy-start.7 = (bf16[192,192]{1,0:T(8,128)(2,1)S(1)}, bf16[192,192]{1,0:T(8,128)(2,1)}, u32[]{:S(2)}) copy-start(bf16[192,192]{1,0:T(8,128)(2,1)} %constant.5.clone.z_table_ref) | copy-start | bytes 221188

commit v2 on v0

v2 whole, which is shorter than its diff:
```python
import functools
import math

import jax
import jax.numpy as jnp
import ml_dtypes
import numpy as np
from jax import lax
from jax.experimental import pallas as pl
from jax.experimental.pallas import tpu as pltpu
from jax.sharding import PartitionSpec as P

C = 32
NG = 384
NXI = 256
WY = 16
RO = 384
P_SIZE = 32
KP = 3
BLKB = 4
CAPK = 4

SMOOTHING = 0.5
GOLDEN_STEP = 40503
TURN_STEPS = 65536

F32 = jnp.float32
BF16 = jnp.bfloat16
LANES = 128
PC = 2 * C
ROUTE_ROWS = KP * PC
HALVES = 2
COIL_GROUPS = 4
GC = C // COIL_GROUPS
MESH = pl.DeviceIdType.MESH
FAR = -1000.0


def iota(shape, dim):
    return lax.broadcasted_iota(jnp.int32, shape, dim)


def turn_waves(turns):
    quarter = jnp.floor(4.0 * turns + 0.5)
    angle = (2.0 * math.pi) * (turns - 0.25 * quarter)
    sq = angle * angle
    sine = angle + angle * sq * (
        -1.0 / 6 + sq * (1.0 / 120 + sq * (-1.0 / 5040 + sq * (1.0 / 362880)))
    )
    cosine = 1.0 + sq * (
        -0.5 + sq * (1.0 / 24 + sq * (-1.0 / 720 + sq * (1.0 / 40320 + sq * (-1.0 / 3628800))))
    )
    turn = quarter - 4.0 * jnp.floor(0.25 * quarter)
    odd = (turn == 1.0) | (turn == 3.0)
    first = jnp.where(odd, sine, cosine)
    second = jnp.where(odd, cosine, sine)
    cos_out = jnp.where((turn == 1.0) | (turn == 2.0), -first, first)
    sin_out = jnp.where(turn >= 2.0, -second, second)
    return cos_out, sin_out


def spline_weight(offset):
    distance = jnp.abs(offset)
    inside = 2.0 / 3.0 + distance * distance * (0.5 * distance - 1.0)
    rest = jnp.maximum(2.0 - distance, 0.0)
    return jnp.where(distance < 1.0, inside, rest * rest * (rest * (1.0 / 6.0)))


def all_bytes(ref, sem):
    pltpu.make_async_copy(ref, ref, sem).wait()


def slab_kernel(
    bins,
    slabs,
    data_hbm,
    route_hbm,
    spoke_hbm,
    segment_hbm,
    count_hbm,
    sens_hbm,
    image_hbm,
    weight_hbm,
    x_table_hbm,
    z_table_hbm,
    out_ref,
    data,
    route,
    spoke,
    segment,
    count,
    sens,
    image,
    weight,
    x_table,
    z_table,
    stacked,
    placed_rows,
    tiles,
    coords,
    tiles_in,
    coords_in,
    above,
    below,
    own_edge,
    samples,
    row_real,
    row_imag,
    across,
    kernel_x,
    weighted,
    sending,
    received,
    widened,
    total,
    load_sems,
    own_sems,
    send_sems,
    recv_sems,
    group_send_sems,
    group_recv_sems,
):
    slab = lax.axis_index("slab")
    me = lax.axis_index("bin")
    half_slabs = slabs // HALVES
    half = lax.div(slab, half_slabs)
    place = lax.rem(slab, half_slabs)
    opposite = lax.rem(slab + half_slabs, slabs)
    sources = HALVES * bins
    parts = HALVES * KP
    depth = KP * slabs
    rows = 2 * NXI // slabs
    wide = out_ref.shape[1]
    blocks = data.shape[0]
    lanes_in = bins * LANES

    barrier = pltpu.get_barrier_semaphore()
    route_peers = [(side, step) for step in range(bins) for side in (1, 0)]
    route_peers.remove((0, 0))

    def route_peer(across_half, step):
        return {
            "bin": lax.rem(me + step, bins),
            "slab": opposite if across_half else slab,
        }

    def half_peer(step):
        return lax.rem(place + step, half_slabs)

    for pair in route_peers:
        pl.semaphore_signal(barrier, inc=1, device_id=route_peer(*pair), device_id_type=MESH)
    for step in range(1, half_slabs):
        pl.semaphore_signal(
            barrier,
            inc=1,
            device_id={"slab": half * half_slabs + half_peer(step)},
            device_id_type=MESH,
        )

    loads = [
        pltpu.make_async_copy(from_ref, to_ref, load_sems.at[at])
        for at, (from_ref, to_ref) in enumerate(
            [
                (route_hbm, route),
                (spoke_hbm, spoke),
                (segment_hbm, segment),
                (count_hbm, count),
                (data_hbm, data),
                (image_hbm, image),
                (weight_hbm, weight),
                (x_table_hbm.at[half], x_table),
                (z_table_hbm, z_table),
                (sens_hbm, sens),
            ]
        )
    ]
    for copy in loads:
        copy.start()
    for copy in loads[:4]:
        copy.wait()

    row = iota((blocks, LANES), 0)
    lane = iota((blocks, LANES), 1)
    lane_block = lane & (blocks - 1)

    def column(ref_row):
        spread = jnp.broadcast_to(ref_row.astype(F32), (blocks, blocks))
        eye = iota((blocks, blocks), 0) == iota((blocks, blocks), 1)
        return jnp.sum(jnp.where(eye, spread, 0.0), axis=1, keepdims=True)

    route_col = jnp.broadcast_to(column(route[...]), (blocks, LANES))
    route_row = jnp.sum(jnp.where(row == lane_block, route_col, 0.0), axis=0, keepdims=True)
    same = route_col == jnp.broadcast_to(route_row, (blocks, LANES))
    rank_row = jnp.sum(jnp.where(same & (row < lane_block), 1.0, 0.0), axis=0, keepdims=True)
    rank_col = jnp.sum(jnp.where(same & (lane < row), 1.0, 0.0), axis=1, keepdims=True)
    slot_row = route_row * CAPK + rank_row

    turn_row = (spoke[...] * GOLDEN_STEP) & (TURN_STEPS - 1)
    columns = [column(turn_row >> 8), column(turn_row & 255), column(segment[...]), column(count[...])]
    slot_hit = rank_col == (lane & (CAPK - 1)).astype(F32)
    picks = [jnp.where(slot_hit, value, 0.0) for value in columns]
    picks = jnp.concatenate(picks, axis=1).astype(BF16)
    picks = jnp.concatenate(
        [picks, jnp.zeros((LANES - blocks, len(columns) * LANES), BF16)], axis=0
    )
    coord_shape = (8 * bins, LANES)
    out_row = iota(coord_shape, 0)
    out_lane = iota(coord_shape, 1)
    part_row = out_row & 7
    is_x = part_row < KP
    partition = jnp.where(is_x, part_row, part_row - KP)
    row_route = jnp.where(part_row < 2 * KP, KP * (out_row >> 3) + partition, -1).astype(F32)
    chosen = (row_route == jnp.broadcast_to(route_row, coord_shape)) & (out_lane < blocks)
    spread = jnp.dot(jnp.where(chosen, 1.0, 0.0).astype(BF16), picks, preferred_element_type=F32)
    turns = (256.0 * spread[:, :LANES] + spread[:, LANES : 2 * LANES]) * (1.0 / TURN_STEPS)
    cosine, sine = turn_waves(turns)
    sample = (2 * ((out_lane & 63) >> 2) + (out_lane >> 6)).astype(F32)
    radial = (P_SIZE * spread[:, 2 * LANES : 3 * LANES] + sample - RO // 2 + 0.5) * ((NG - 8) / RO)
    coord_x = jnp.where(sample < spread[:, 3 * LANES :], NG / 2 + radial * cosine, FAR)
    coord_y = NG / 2 + radial * sine
    coords[...] = jnp.where(is_x, coord_x, coord_y)

    def coord_rows(index):
        return pl.ds(pl.multiple_of(index * 8, 8), 8)

    def tile_rows(index):
        return pl.ds(pl.multiple_of(index * ROUTE_ROWS, ROUTE_ROWS), ROUTE_ROWS)

    my_source = half * bins + me
    image_copy = pltpu.make_async_remote_copy(
        image,
        above,
        send_sems.at[2],
        recv_sems.at[2],
        {"bin": lax.rem(me + bins - 1, bins)},
        MESH,
    )
    edge_copy = pltpu.make_async_remote_copy(
        own_edge, below, send_sems.at[3], recv_sems.at[3], {"bin": lax.rem(me + 1, bins)}, MESH
    )
    is_first = me == 0
    is_last = me == bins - 1
    loads[5].wait()
    pl.semaphore_wait(barrier, len(route_peers) + half_slabs - 1)

    @pl.when(jnp.logical_not(is_first))
    def _():
        image_copy.start()

    for pair in route_peers:
        peer = route_peer(*pair)
        pltpu.make_async_remote_copy(
            coords.at[coord_rows(peer["bin"])],
            coords_in.at[coord_rows(my_source)],
            send_sems.at[0],
            recv_sems.at[0],
            peer,
            MESH,
        ).start()
    own_coords = pltpu.make_async_copy(
        coords.at[coord_rows(me)], coords_in.at[coord_rows(my_source)], own_sems.at[0]
    )
    own_coords.start()

    loads[4].wait()
    big = (bins * KP * 16, LANES)
    place_row = iota(big, 0)
    place_lane = iota(big, 1)
    wanted = (CAPK * (place_row >> 4) + (place_row & 3)).astype(F32)
    hit = (wanted == jnp.broadcast_to(slot_row, big)) & (((place_row >> 2) & 3) == (place_lane >> 5))
    one_hot = jnp.where(hit, 1.0, 0.0).astype(BF16)
    for quarter in range(4):
        for fourth in range(4):
            first = (4 * fourth + quarter) * LANES
            to_rows = slice(quarter * blocks, (quarter + 1) * blocks)
            stacked[to_rows, fourth * LANES : (fourth + 1) * LANES] = data[:, first : first + LANES]
    placed_rows[...] = jnp.dot(one_hot, stacked[...], preferred_element_type=F32)
    half_lane = iota((PC, LANES), 1) < 64

    def turn_pair(pair, carry):
        base = pl.multiple_of(pair * 32, 32)
        pieces = [
            placed_rows[pl.ds(base + 16 * one, 16), fourth * LANES : (fourth + 1) * LANES]
            for one in range(2)
            for fourth in range(4)
        ]
        turned = jnp.concatenate(pieces, axis=0).T
        low, high = turned[:PC], turned[PC:]
        at = pl.multiple_of(pair * 2 * PC, 2 * PC)
        tiles[pl.ds(at, PC), :] = jnp.where(half_lane, low, pltpu.roll(high, 64, 1)).astype(BF16)
        tiles[pl.ds(at + PC, PC), :] = jnp.where(half_lane, pltpu.roll(low, 64, 1), high).astype(BF16)
        return carry

    lax.fori_loop(0, bins * KP // 2, turn_pair, 0)
    for pair in route_peers:
        peer = route_peer(*pair)
        pltpu.make_async_remote_copy(
            tiles.at[tile_rows(peer["bin"])],
            tiles_in.at[tile_rows(my_source)],
            send_sems.at[1],
            recv_sems.at[1],
            peer,
            MESH,
        ).start()
    own_tiles = pltpu.make_async_copy(
        tiles.at[tile_rows(me)], tiles_in.at[tile_rows(my_source)], own_sems.at[1]
    )
    own_tiles.start()

    own_coords.wait()
    others = pl.ds(0, (sources - 1) * 8)
    all_bytes(coords_in.at[others], recv_sems.at[0])
    loads[7].wait()
    y_offset = (iota((WY, LANES), 0) - WY // 2).astype(F32)
    taps = [turn_waves(y_offset * (m / NG)) for m in range(1, 4)]

    def prepare(step, carry):
        side = lax.div(step, KP)
        part = lax.rem(step, KP)

        def prepare_source(source, carry):
            base = pl.multiple_of((side * bins + source) * 8, 8)
            coord_x = coords_in[pl.ds(base + part, 1), :]
            coord_y = coords_in[pl.ds(base + KP + part, 1), :]
            cell = jnp.floor(coord_y)
            ahead = coord_y - cell
            behind = 1.0 - ahead
            weights = [
                behind * behind * behind * (1.0 / 6.0),
                2.0 / 3.0 + ahead * ahead * (0.5 * ahead - 1.0),
                2.0 / 3.0 + behind * behind * (0.5 * behind - 1.0),
                ahead * ahead * ahead * (1.0 / 6.0),
            ]
            steps = y_offset * (cell - (1.0 + NG // 2))
            base_turns = steps * (1.0 / NG)
            base_cos, base_sin = turn_waves(base_turns - jnp.floor(base_turns))
            sum_cos = jnp.broadcast_to(weights[0], (WY, LANES))
            sum_sin = jnp.zeros((WY, LANES), F32)
            for tap_weight, (tap_cos, tap_sin) in zip(weights[1:], taps):
                sum_cos = sum_cos + tap_weight * tap_cos
                sum_sin = sum_sin + tap_weight * tap_sin
            at = pl.ds(pl.multiple_of((step * bins + source) * WY, WY), WY)
            row_real[at, :] = sum_cos * base_cos - sum_sin * base_sin
            row_imag[at, :] = sum_cos * base_sin + sum_sin * base_cos
            lanes = pl.ds(pl.multiple_of(source * LANES, LANES), LANES)
            piece = 32
            for first in range(0, NG, piece):
                cells = (iota((piece, LANES), 0) + first).astype(F32)
                across[first : first + piece, lanes] = spline_weight(coord_x - cells).astype(BF16)
            return carry

        lax.fori_loop(0, bins, prepare_source, 0)
        kernel_x[step] = jnp.dot(x_table[...], across[...], preferred_element_type=F32).astype(BF16)
        return carry

    lax.fori_loop(0, parts, prepare, 0)

    loads[6].wait()

    @pl.when(jnp.logical_not(is_last))
    def _():
        image_copy.wait_recv()

    @pl.when(is_last)
    def _():
        above[...] = image[...]

    lane = iota((depth, wide), 1)
    upper_half = ((lane >> 4) & 1) == 1
    from_lane = iota((wide // 2, wide), 0)
    to_lane = iota((wide // 2, wide), 1)
    widen_weight = jnp.where(from_lane == ((to_lane >> 5) << 4) + (to_lane & 15), 1.0, 0.0)
    difference = above[...] - image[...]
    square = difference * difference
    other = jnp.where(upper_half, pltpu.roll(square, 16, 1), pltpu.roll(square, wide - 16, 1))
    magnitude = jnp.sqrt(square + other + SMOOTHING * SMOOTHING)
    wide_weight = jnp.dot(
        weight[...], widen_weight, preferred_element_type=F32, precision=lax.Precision.HIGHEST
    )
    own_edge[...] = wide_weight * difference / magnitude

    @pl.when(jnp.logical_not(is_last))
    def _():
        edge_copy.start()

    @pl.when(is_first)
    def _():
        below[...] = jnp.zeros_like(below)

    own_tiles.wait()
    others = pl.ds(0, (sources - 1) * ROUTE_ROWS)
    all_bytes(tiles_in.at[others], recv_sems.at[1])

    def widen_samples(source, carry):
        samples[source] = tiles_in[tile_rows(source), :].astype(F32)
        return carry

    lax.fori_loop(0, sources, widen_samples, 0)

    def own_copy(group):
        return pltpu.make_async_copy(
            sending.at[group, place], received.at[group, place], own_sems.at[2 + group]
        )

    for group in range(COIL_GROUPS):

        def grid_part(step, carry, group=group):
            side = lax.div(step, KP)
            part = lax.rem(step, KP)

            def weigh(source, carry):
                at = pl.ds(pl.multiple_of((step * bins + source) * WY, WY), WY)
                real, imag = row_real[at, :], row_imag[at, :]
                lanes = pl.ds(pl.multiple_of(source * LANES, LANES), LANES)
                for coil in range(GC):
                    at_row = part * PC + group * GC + coil
                    data_real = samples[side * bins + source, pl.ds(at_row, 1), :]
                    data_imag = samples[side * bins + source, pl.ds(at_row + C, 1), :]
                    weighted[coil * WY : (coil + 1) * WY, lanes] = (
                        real * data_real - imag * data_imag
                    ).astype(BF16)
                    weighted[(GC + coil) * WY : (GC + coil + 1) * WY, lanes] = (
                        real * data_imag + imag * data_real
                    ).astype(BF16)
                return carry

            lax.fori_loop(0, bins, weigh, 0)
            products = lax.dot_general(
                kernel_x[step],
                weighted[...],
                (((1,), (1,)), ((), ())),
                preferred_element_type=F32,
            )
            count_x = NXI // HALVES
            real = products[:count_x, :LANES] - products[count_x:, LANES:]
            imag = products[:count_x, LANES:] + products[count_x:, :LANES]
            shape = (half_slabs, rows // 2, LANES)
            spectra = jnp.concatenate([real.reshape(shape), imag.reshape(shape)], axis=1)
            at = pl.ds(pl.multiple_of(step * rows, rows), rows)
            sending[group, :, at, :] = spectra.astype(BF16)
            return carry

        lax.fori_loop(0, parts, grid_part, 0)
        for step in range(1, half_slabs):
            peer = half_peer(step)
            pltpu.make_async_remote_copy(
                sending.at[group, peer],
                received.at[group, place],
                group_send_sems.at[group],
                group_recv_sems.at[group],
                {"slab": half * half_slabs + peer},
                MESH,
            ).start()
        own_copy(group).start()

    loads[8].wait()
    loads[9].wait()
    features = GC * WY
    for group in range(COIL_GROUPS):
        own_copy(group).wait()
        others = pl.ds(0, half_slabs - 1)
        all_bytes(received.at[group, others], group_recv_sems.at[group])

        def widen(source, carry, group=group):
            at = pl.ds(source * parts, parts)
            widened[at] = received[group, source].astype(F32).reshape(parts, rows, LANES)
            return carry

        lax.fori_loop(0, half_slabs, widen, 0)
        for pair in range(rows // 4):
            inputs = []
            for at_x in (2 * pair, 2 * pair + 1):
                real = widened[:, at_x, :].astype(BF16)
                imag = widened[:, rows // 2 + at_x, :].astype(BF16)
                inputs.append(jnp.concatenate([real, imag], axis=0))
            images = jnp.dot(
                z_table[...], jnp.concatenate(inputs, axis=1), preferred_element_type=F32
            )
            for at, at_x in enumerate((2 * pair, 2 * pair + 1)):
                image_real = images[:depth, at * LANES : (at + 1) * LANES]
                image_imag = images[depth:, at * LANES : (at + 1) * LANES]
                first = 2 * at_x * C * WY + group * features
                sens_real = sens[:, first : first + features].astype(F32)
                first = first + C * WY
                sens_imag = sens[:, first : first + features].astype(F32)
                real = sens_real * image_real + sens_imag * image_imag
                imag = sens_real * image_imag - sens_imag * image_real
                if group > 0:
                    real = real + total[2 * at_x]
                    imag = imag + total[2 * at_x + 1]
                total[2 * at_x] = real
                total[2 * at_x + 1] = imag

    others = pl.ds(0, half_slabs - 1)
    for group in range(COIL_GROUPS):
        all_bytes(sending.at[group, others], group_send_sems.at[group])
    all_bytes(coords_in.at[pl.ds(0, (sources - 1) * 8)], send_sems.at[0])
    all_bytes(tiles_in.at[pl.ds(0, (sources - 1) * ROUTE_ROWS)], send_sems.at[1])

    @pl.when(jnp.logical_not(is_first))
    def _():
        image_copy.wait_send()
        edge_copy.wait_recv()

    @pl.when(jnp.logical_not(is_last))
    def _():
        edge_copy.wait_send()

    scaling = 1.0 / math.sqrt(P_SIZE * bins * BLKB * depth * C / KP)
    octet = iota((depth, LANES), 1) >> 4
    for part in range(rows // 8):
        line = jnp.zeros((depth, LANES), F32)
        for at in range(8):
            value = total[part * 8 + at]
            for shift in (64, 32, 16):
                value = value + pltpu.roll(value, shift, 1)
            line = jnp.where(octet == at, value, line)
        lanes = slice(part * LANES, (part + 1) * LANES)
        out_ref[:, lanes] = below[:, lanes] - own_edge[:, lanes] - line * scaling


def slab_gradient(
    bins, slabs, data, route, spoke, segment, count, sens, image, weight, x_table, z_table
):
    hbm = pl.BlockSpec(memory_space=pltpu.HBM)
    depth = sens.shape[0]
    blocks = data.shape[0]
    rows = 2 * NXI // slabs
    sources = HALVES * bins
    parts = HALVES * KP
    half_slabs = slabs // HALVES
    operands = (data, route, spoke, segment, count, sens, image, weight, x_table, z_table)
    held = operands[:8] + (x_table[0], z_table)
    return pl.pallas_call(
        functools.partial(slab_kernel, bins, slabs),
        out_shape=jax.ShapeDtypeStruct(image.shape, F32),
        in_specs=[hbm] * len(operands),
        out_specs=pl.BlockSpec(memory_space=pltpu.VMEM),
        scratch_shapes=[pltpu.VMEM(array.shape, array.dtype) for array in held]
        + [
            pltpu.VMEM((4 * blocks, 4 * LANES), BF16),
            pltpu.VMEM((bins * KP * 16, 4 * LANES), F32),
            pltpu.VMEM((bins * ROUTE_ROWS, LANES), BF16),
            pltpu.VMEM((bins * 8, LANES), F32),
            pltpu.VMEM((sources * ROUTE_ROWS, LANES), BF16),
            pltpu.VMEM((sources * 8, LANES), F32),
            pltpu.VMEM(image.shape, F32),
            pltpu.VMEM(image.shape, F32),
            pltpu.VMEM(image.shape, F32),
            pltpu.VMEM((sources, ROUTE_ROWS, LANES), F32),
            pltpu.VMEM((parts * bins * WY, LANES), F32),
            pltpu.VMEM((parts * bins * WY, LANES), F32),
            pltpu.VMEM((NG, bins * LANES), BF16),
            pltpu.VMEM((parts, 2 * NXI // HALVES, bins * LANES), BF16),
            pltpu.VMEM((2 * GC * WY, bins * LANES), BF16),
            pltpu.VMEM((COIL_GROUPS, half_slabs, parts * rows, LANES), BF16),
            pltpu.VMEM((COIL_GROUPS, half_slabs, parts * rows, LANES), BF16),
            pltpu.VMEM((depth, rows, LANES), F32),
            pltpu.VMEM((rows, depth, LANES), F32),
            pltpu.SemaphoreType.DMA((len(operands),)),
            pltpu.SemaphoreType.DMA((2 + COIL_GROUPS,)),
            pltpu.SemaphoreType.DMA((4,)),
            pltpu.SemaphoreType.DMA((4,)),
            pltpu.SemaphoreType.DMA((COIL_GROUPS,)),
            pltpu.SemaphoreType.DMA((COIL_GROUPS,)),
        ],
        compiler_params=pltpu.CompilerParams(
            collective_id=0, has_side_effects=True, vmem_limit_bytes=48 << 20
        ),
    )(*operands)


def waves(out_index, in_index, modulus):
    angles = 2.0 * math.pi / modulus * (out_index[:, None] * in_index[None, :] % modulus)
    return np.cos(angles), np.sin(angles)


def x_phases():
    cosine, sine = waves(np.arange(NXI) - NXI // 2, np.arange(NG) - NG // 2, NG)
    shape = (HALVES, NXI // HALVES, NG)
    return np.concatenate([cosine.reshape(shape), sine.reshape(shape)], axis=1)


def z_phases(slabs):
    depth = KP * slabs
    order = np.arange(depth).reshape(HALVES, slabs // HALVES, KP).transpose(1, 0, 2).reshape(-1)
    cosine, sine = waves(np.arange(depth) - depth // 2, order - depth // 2, depth)
    return np.concatenate(
        [np.concatenate([cosine, -sine], axis=1), np.concatenate([sine, cosine], axis=1)], axis=0
    )


def shards(
    sample_data,
    block_route,
    spoke_index,
    segment_index,
    sample_count,
    sensitivity,
    image,
    tv_weight,
):
    bins = lax.axis_size("bin")
    slabs = lax.axis_size("slab")
    gradient = slab_gradient(
        bins,
        slabs,
        sample_data,
        block_route.reshape(1, -1),
        spoke_index.reshape(1, -1),
        segment_index.reshape(1, -1),
        sample_count.reshape(1, -1),
        sensitivity,
        image[0],
        tv_weight[0],
        jnp.asarray(x_phases().astype(ml_dtypes.bfloat16)),
        jnp.asarray(z_phases(slabs).astype(ml_dtypes.bfloat16)),
    )
    return gradient.reshape(image.shape)


def solution(mesh):
    return jax.shard_map(
        shards,
        mesh=mesh,
        in_specs=(
            P(("bin", "slab"), None),
            P(("bin", "slab"), None),
            P(("bin", "slab")),
            P(("bin", "slab")),
            P(("bin", "slab")),
            P(None, "slab"),
            P("bin", None, "slab"),
            P("bin", None, "slab"),
        ),
        out_specs=P("bin", None, "slab"),
        check_vma=False,
    )
```

time: 304 us -> 69.1 us (0.23)
  the two profiles are of different devices: /device:TPU:1 before, /device:TPU:7 now
where the time goes in v2:
time: 69.1 us; the launch traced here: 68.8 us
  Pallas kernels  59.6 us (86%)
  local copies, waits for them, and re-layouts  9.15 us (13%)
    pallas_call x1, Pallas kernels, slab_gradient(): pl.pallas_call(functools.partial(slab_kernel, bins, slabs), out_shape=jax...  59.6 us
    unnamed x21, local copies, waits for them, and re-layouts  9.15 us

profile of v2, /device:TPU:7, one launch (start us, length us, event | category | flops | bytes accessed | tf_op | source)
XLA Modules:
  0.0 68.8 jit_solution(6755528334109355)
XLA Ops:
  0.0 0.0 copy-start
  0.0 1.4 %copy-done = bf16[96,8192]{1,0:T(8,128)(2,1)S(1)} copy-done((bf16[96,8192]{1,0:T(8,128)(2,1)S(1)}, bf16[96,8192]{1,0:T(8,128)(2,1)}, u32[]{:S(2)}) %copy-start) | copy-done | bytes 1572888
  1.4 0.0 copy-start.1
  1.4 1.0 %copy-done.1 = bf16[2,256,384]{2,1,0:T(8,128)(2,1)S(1)} copy-done((bf16[2,256,384]{2,1,0:T(8,128)(2,1)S(1)}, bf16[2,256,384]{2,1,0:T(8,128)(2,1)}, u32[]{:S(2)}) %copy-start.1) | copy-done | bytes 393240
  2.4 0.0 copy-start.2
  2.4 0.9 %copy-done.2 = bf16[32,2048]{1,0:T(8,128)(2,1)S(1)} copy-done((bf16[32,2048]{1,0:T(8,128)(2,1)S(1)}, bf16[32,2048]{1,0:T(8,128)(2,1)}, u32[]{:S(2)}) %copy-start.2) | copy-done | bytes 131096
  3.3 0.0 copy-start.3
  3.3 0.9 %copy-done.3 = f32[1,96,256]{2,1,0:T(8,128)S(1)} copy-done((f32[1,96,256]{2,1,0:T(8,128)S(1)}, f32[1,96,256]{2,1,0:T(8,128)}, u32[]{:S(2)}) %copy-start.3) | copy-done | bytes 98328
  4.2 0.0 copy-start.4
  4.2 0.9 %copy-done.4 = bf16[192,192]{1,0:T(8,128)(2,1)S(1)} copy-done((bf16[192,192]{1,0:T(8,128)(2,1)S(1)}, bf16[192,192]{1,0:T(8,128)(2,1)}, u32[]{:S(2)}) %copy-start.4) | copy-done | bytes 73752
  5.1 0.0 copy-start.5
  5.1 0.8 %copy-done.5 = f32[1,96,128]{2,1,0:T(8,128)S(1)} copy-done((f32[1,96,128]{2,1,0:T(8,128)S(1)}, f32[1,96,128]{2,1,0:T(8,128)}, u32[]{:S(2)}) %copy-start.5) | copy-done | bytes 49176
  5.9 0.0 copy-start.6
  5.9 0.7 copy-done.6
  6.6 0.0 copy-start.7
  6.6 0.7 copy-done.7
  7.2 0.0 copy-start.8
  7.2 0.7 copy-done.8
  7.9 0.0 copy-start.9
  7.9 0.7 copy-done.9
  8.5 59.6 %shard_map.100 = f32[96,256]{1,0:T(8,128)S(1)} custom-call(bf16[32,2048]{1,0:T(8,128)(2,1)S(1)} %copy-done.2, s32[1,32]{1,0:T(1,128)S(1)} %bitcast.10, s32[1,32]{1,0:T(1,128)S(1)} %bitcast.11, s32[1,32]{1,0:T(1,128)S(1)} %bitcast.12, s32[1,32]{1,0:T(1,128)S(1)} %bitcast.13, bf16[96,8192]{1,0:T(8,128)(2,1)S(1)} %copy-done, f32[96,256]{1,0:T(8,128)S(1)} %bitcast.8, ...), custom_call_target="tpu_custom_call" | custom-call | tf_op jit(solution)/shard_map/pallas_call | solution.py:534
  68.1 0.6 copy.12
Async XLA Ops:
  0.0 1.4 %copy-start = (bf16[96,8192]{1,0:T(8,128)(2,1)S(1)}, bf16[96,8192]{1,0:T(8,128)(2,1)}, u32[]{:S(2)}) copy-start(bf16[96,8192]{1,0:T(8,128)(2,1)} %sens_hbm.1) | copy-start | bytes 4718596
  1.4 1.0 %copy-start.1 = (bf16[2,256,384]{2,1,0:T(8,128)(2,1)S(1)}, bf16[2,256,384]{2,1,0:T(8,128)(2,1)}, u32[]{:S(2)}) copy-start(bf16[2,256,384]{2,1,0:T(8,128)(2,1)} %constant.4.clone.x_table_hbm) | copy-start | bytes 1179652
  2.4 0.9 %copy-start.2 = (bf16[32,2048]{1,0:T(8,128)(2,1)S(1)}, bf16[32,2048]{1,0:T(8,128)(2,1)}, u32[]{:S(2)}) copy-start(bf16[32,2048]{1,0:T(8,128)(2,1)} %data_hbm.1) | copy-start | bytes 393220
  3.3 0.9 %copy-start.3 = (f32[1,96,256]{2,1,0:T(8,128)S(1)}, f32[1,96,256]{2,1,0:T(8,128)}, u32[]{:S(2)}) copy-start(f32[1,96,256]{2,1,0:T(8,128)} %param.16) | copy-start | bytes 294916
  4.2 0.9 %copy-start.4 = (bf16[192,192]{1,0:T(8,128)(2,1)S(1)}, bf16[192,192]{1,0:T(8,128)(2,1)}, u32[]{:S(2)}) copy-start(bf16[192,192]{1,0:T(8,128)(2,1)} %constant.5.clone.z_table_hbm) | copy-start | bytes 221188
  5.1 0.8 %copy-start.5 = (f32[1,96,128]{2,1,0:T(8,128)S(1)}, f32[1,96,128]{2,1,0:T(8,128)}, u32[]{:S(2)}) copy-start(f32[1,96,128]{2,1,0:T(8,128)} %param.17) | copy-start | bytes 147460
  5.9 0.7 copy-start.6
  6.6 0.7 copy-start.7
  7.2 0.7 copy-start.8
  7.9 0.7 copy-start.9

commit v3 on v2

--- a/solution.py
+++ b/solution.py
@@ -109,14 +109,18 @@
     across,
     kernel_x,
     weighted,
+    products,
     sending,
     received,
     widened,
     total,
+    fold,
     load_sems,
     own_sems,
     send_sems,
     recv_sems,
+    tile_send_sems,
+    tile_recv_sems,
     group_send_sems,
     group_recv_sems,
 ):
@@ -132,7 +136,6 @@
     rows = 2 * NXI // slabs
     wide = out_ref.shape[1]
     blocks = data.shape[0]
-    lanes_in = bins * LANES
 
     barrier = pltpu.get_barrier_semaphore()
     route_peers = [(side, step) for step in range(bins) for side in (1, 0)]
@@ -223,20 +226,20 @@
     def coord_rows(index):
         return pl.ds(pl.multiple_of(index * 8, 8), 8)
 
-    def tile_rows(index):
-        return pl.ds(pl.multiple_of(index * ROUTE_ROWS, ROUTE_ROWS), ROUTE_ROWS)
+    def tile_rows(index, many=1):
+        return pl.ds(pl.multiple_of(index * PC, PC), many * PC)
 
     my_source = half * bins + me
     image_copy = pltpu.make_async_remote_copy(
         image,
         above,
-        send_sems.at[2],
-        recv_sems.at[2],
+        send_sems.at[1],
+        recv_sems.at[1],
         {"bin": lax.rem(me + bins - 1, bins)},
         MESH,
     )
     edge_copy = pltpu.make_async_remote_copy(
-        own_edge, below, send_sems.at[3], recv_sems.at[3], {"bin": lax.rem(me + 1, bins)}, MESH
+        own_edge, below, send_sems.at[2], recv_sems.at[2], {"bin": lax.rem(me + 1, bins)}, MESH
     )
     is_first = me == 0
     is_last = me == bins - 1
@@ -292,20 +295,29 @@
         return carry
 
     lax.fori_loop(0, bins * KP // 2, turn_pair, 0)
-    for pair in route_peers:
-        peer = route_peer(*pair)
-        pltpu.make_async_remote_copy(
-            tiles.at[tile_rows(peer["bin"])],
-            tiles_in.at[tile_rows(my_source)],
-            send_sems.at[1],
-            recv_sems.at[1],
-            peer,
-            MESH,
-        ).start()
-    own_tiles = pltpu.make_async_copy(
-        tiles.at[tile_rows(me)], tiles_in.at[tile_rows(my_source)], own_sems.at[1]
-    )
-    own_tiles.start()
+    own_tiles = []
+    for part in range(KP):
+        slot = part * sources + my_source
+        for pair in route_peers:
+            peer = route_peer(*pair)
+            pltpu.make_async_remote_copy(
+                tiles.at[tile_rows(peer["bin"] * KP + part)],
+                tiles_in.at[tile_rows(slot)],
+                tile_send_sems.at[part],
+                tile_recv_sems.at[part],
+                peer,
+                MESH,
+            ).start()
+        copy = pltpu.make_async_copy(
+            tiles.at[tile_rows(me * KP + part)], tiles_in.at[tile_rows(slot)], own_sems.at[1 + part]
+        )
+        copy.start()
+        own_tiles.append(copy)
+
+    fold_row = iota(fold.shape, 0)
+    fold_lane = iota(fold.shape, 1)
+    folds = ((fold_lane >> 4) == (fold_row >> 7)) & ((fold_lane & 15) == (fold_row & 15))
+    fold[...] = jnp.where(folds, 1.0, 0.0).astype(BF16)
 
     own_coords.wait()
     others = pl.ds(0, (sources - 1) * 8)
@@ -343,14 +355,14 @@
             row_real[at, :] = sum_cos * base_cos - sum_sin * base_sin
             row_imag[at, :] = sum_cos * base_sin + sum_sin * base_cos
             lanes = pl.ds(pl.multiple_of(source * LANES, LANES), LANES)
-            piece = 32
-            for first in range(0, NG, piece):
-                cells = (iota((piece, LANES), 0) + first).astype(F32)
-                across[first : first + piece, lanes] = spline_weight(coord_x - cells).astype(BF16)
+            turned = jnp.broadcast_to(coord_x, (LANES, LANES)).T
+            for first in range(0, NG, LANES):
+                cells = (iota((LANES, LANES), 1) + first).astype(F32)
+                across[lanes, first : first + LANES] = spline_weight(turned - cells).astype(BF16)
             return carry
 
         lax.fori_loop(0, bins, prepare_source, 0)
-        kernel_x[step] = jnp.dot(x_table[...], across[...], preferred_element_type=F32).astype(BF16)
+        kernel_x[step] = jnp.dot(across[...], x_table[...], preferred_element_type=F32).astype(BF16)
         return carry
 
     lax.fori_loop(0, parts, prepare, 0)
@@ -387,60 +399,74 @@
     def _():
         below[...] = jnp.zeros_like(below)
 
-    own_tiles.wait()
-    others = pl.ds(0, (sources - 1) * ROUTE_ROWS)
-    all_bytes(tiles_in.at[others], recv_sems.at[1])
-
-    def widen_samples(source, carry):
-        samples[source] = tiles_in[tile_rows(source), :].astype(F32)
-        return carry
-
-    lax.fori_loop(0, sources, widen_samples, 0)
-
     def own_copy(group):
         return pltpu.make_async_copy(
-            sending.at[group, place], received.at[group, place], own_sems.at[2 + group]
+            sending.at[group, place], received.at[group, place], own_sems.at[1 + KP + group]
         )
 
-    for group in range(COIL_GROUPS):
-
-        def grid_part(step, carry, group=group):
-            side = lax.div(step, KP)
-            part = lax.rem(step, KP)
+    def take_tiles(part):
+        own_tiles[part].wait()
+        others = tile_rows(part * sources, sources - 1)
+        all_bytes(tiles_in.at[others], tile_recv_sems.at[part])
+
+        def widen_samples(source, carry):
+            samples[source] = tiles_in[tile_rows(part * sources + source), :].astype(F32)
+            return carry
+
+        lax.fori_loop(0, sources, widen_samples, 0)
+
+    count_x = NXI // HALVES
+    group_rows = 2 * GC * WY
+
+    def grid_part(part, groups):
+        def one_side(side, carry):
+            step = side * KP + part
 
             def weigh(source, carry):
                 at = pl.ds(pl.multiple_of((step * bins + source) * WY, WY), WY)
                 real, imag = row_real[at, :], row_imag[at, :]
                 lanes = pl.ds(pl.multiple_of(source * LANES, LANES), LANES)
-                for coil in range(GC):
-                    at_row = part * PC + group * GC + coil
-                    data_real = samples[side * bins + source, pl.ds(at_row, 1), :]
-                    data_imag = samples[side * bins + source, pl.ds(at_row + C, 1), :]
-                    weighted[coil * WY : (coil + 1) * WY, lanes] = (
-                        real * data_real - imag * data_imag
-                    ).astype(BF16)
-                    weighted[(GC + coil) * WY : (GC + coil + 1) * WY, lanes] = (
-                        real * data_imag + imag * data_real
-                    ).astype(BF16)
+                for at_group, group in enumerate(groups):
+                    for coil in range(GC):
+                        row = group * GC + coil
+                        data_real = samples[side * bins + source, row : row + 1, :]
+                        data_imag = samples[side * bins + source, row + C : row + C + 1, :]
+                        first = at_group * group_rows + coil * WY
+                        weighted[first : first + WY, lanes] = (
+                            real * data_real - imag * data_imag
+                        ).astype(BF16)
+                        first = first + GC * WY
+                        weighted[first : first + WY, lanes] = (
+                            real * data_imag + imag * data_real
+                        ).astype(BF16)
                 return carry
 
             lax.fori_loop(0, bins, weigh, 0)
-            products = lax.dot_general(
+            products[: len(groups) * group_rows, :] = jnp.dot(
+                weighted[: len(groups) * group_rows, :],
                 kernel_x[step],
-                weighted[...],
-                (((1,), (1,)), ((), ())),
                 preferred_element_type=F32,
             )
-            count_x = NXI // HALVES
-            real = products[:count_x, :LANES] - products[count_x:, LANES:]
-            imag = products[:count_x, LANES:] + products[count_x:, :LANES]
             shape = (half_slabs, rows // 2, LANES)
-            spectra = jnp.concatenate([real.reshape(shape), imag.reshape(shape)], axis=1)
             at = pl.ds(pl.multiple_of(step * rows, rows), rows)
-            sending[group, :, at, :] = spectra.astype(BF16)
+            for at_group, group in enumerate(groups):
+                first = at_group * group_rows
+                above_rows = slice(first, first + group_rows // 2)
+                below_rows = slice(first + group_rows // 2, first + group_rows)
+                real = products[above_rows, :count_x] - products[below_rows, count_x:]
+                imag = products[below_rows, :count_x] + products[above_rows, count_x:]
+                spectra = jnp.concatenate([real.T.reshape(shape), imag.T.reshape(shape)], axis=1)
+                sending[group, :, at, :] = spectra.astype(BF16)
             return carry
 
-        lax.fori_loop(0, parts, grid_part, 0)
+        lax.fori_loop(0, HALVES, one_side, 0)
+
+    for part in range(KP - 1):
+        take_tiles(part)
+        grid_part(part, tuple(range(COIL_GROUPS)))
+    take_tiles(KP - 1)
+    for group in range(COIL_GROUPS):
+        grid_part(KP - 1, (group,))
         for step in range(1, half_slabs):
             peer = half_peer(step)
             pltpu.make_async_remote_copy(
@@ -495,7 +521,8 @@
     for group in range(COIL_GROUPS):
         all_bytes(sending.at[group, others], group_send_sems.at[group])
     all_bytes(coords_in.at[pl.ds(0, (sources - 1) * 8)], send_sems.at[0])
-    all_bytes(tiles_in.at[pl.ds(0, (sources - 1) * ROUTE_ROWS)], send_sems.at[1])
+    for part in range(KP):
+        all_bytes(tiles_in.at[tile_rows(0, sources - 1)], tile_send_sems.at[part])
 
     @pl.when(jnp.logical_not(is_first))
     def _():
@@ -507,15 +534,13 @@
         edge_copy.wait_send()
 
     scaling = 1.0 / math.sqrt(P_SIZE * bins * BLKB * depth * C / KP)
-    octet = iota((depth, LANES), 1) >> 4
     for part in range(rows // 8):
-        line = jnp.zeros((depth, LANES), F32)
-        for at in range(8):
-            value = total[part * 8 + at]
-            for shift in (64, 32, 16):
-                value = value + pltpu.roll(value, shift, 1)
-            line = jnp.where(octet == at, value, line)
         lanes = slice(part * LANES, (part + 1) * LANES)
+        value = jnp.concatenate([total[part * 8 + at] for at in range(8)], axis=1)
+        high = value.astype(BF16)
+        low = (value - high.astype(F32)).astype(BF16)
+        line = jnp.dot(high, fold[...], preferred_element_type=F32)
+        line = line + jnp.dot(low, fold[...], preferred_element_type=F32)
         out_ref[:, lanes] = below[:, lanes] - own_edge[:, lanes] - line * scaling
 
 
@@ -547,25 +572,29 @@
             pltpu.VMEM(image.shape, F32),
             pltpu.VMEM(image.shape, F32),
             pltpu.VMEM(image.shape, F32),
-            pltpu.VMEM((sources, ROUTE_ROWS, LANES), F32),
+            pltpu.VMEM((sources, PC, LANES), F32),
             pltpu.VMEM((parts * bins * WY, LANES), F32),
             pltpu.VMEM((parts * bins * WY, LANES), F32),
-            pltpu.VMEM((NG, bins * LANES), BF16),
-            pltpu.VMEM((parts, 2 * NXI // HALVES, bins * LANES), BF16),
-            pltpu.VMEM((2 * GC * WY, bins * LANES), BF16),
+            pltpu.VMEM((bins * LANES, NG), BF16),
+            pltpu.VMEM((parts, bins * LANES, 2 * NXI // HALVES), BF16),
+            pltpu.VMEM((2 * C * WY, bins * LANES), BF16),
+            pltpu.VMEM((2 * C * WY, 2 * NXI // HALVES), F32),
             pltpu.VMEM((COIL_GROUPS, half_slabs, parts * rows, LANES), BF16),
             pltpu.VMEM((COIL_GROUPS, half_slabs, parts * rows, LANES), BF16),
             pltpu.VMEM((depth, rows, LANES), F32),
             pltpu.VMEM((rows, depth, LANES), F32),
+            pltpu.VMEM((8 * LANES, LANES), BF16),
             pltpu.SemaphoreType.DMA((len(operands),)),
-            pltpu.SemaphoreType.DMA((2 + COIL_GROUPS,)),
-            pltpu.SemaphoreType.DMA((4,)),
-            pltpu.SemaphoreType.DMA((4,)),
+            pltpu.SemaphoreType.DMA((1 + KP + COIL_GROUPS,)),
+            pltpu.SemaphoreType.DMA((3,)),
+            pltpu.SemaphoreType.DMA((3,)),
+            pltpu.SemaphoreType.DMA((KP,)),
+            pltpu.SemaphoreType.DMA((KP,)),
             pltpu.SemaphoreType.DMA((COIL_GROUPS,)),
             pltpu.SemaphoreType.DMA((COIL_GROUPS,)),
         ],
         compiler_params=pltpu.CompilerParams(
-            collective_id=0, has_side_effects=True, vmem_limit_bytes=48 << 20
+            collective_id=0, has_side_effects=True, vmem_limit_bytes=60 << 20
         ),
     )(*operands)
 
@@ -578,7 +607,8 @@
 def x_phases():
     cosine, sine = waves(np.arange(NXI) - NXI // 2, np.arange(NG) - NG // 2, NG)
     shape = (HALVES, NXI // HALVES, NG)
-    return np.concatenate([cosine.reshape(shape), sine.reshape(shape)], axis=1)
+    table = np.concatenate([cosine.reshape(shape), sine.reshape(shape)], axis=1)
+    return table.transpose(0, 2, 1)
 
 
 def z_phases(slabs):

time: 69.1 us -> 59 us (0.85)
  the two profiles are of different devices: /device:TPU:7 before, /device:TPU:1 now
where the time goes in v3:
time: 59 us; the launch traced here: 58.7 us
  Pallas kernels  57.2 us (97%)
  local copies, waits for them, and re-layouts  1.54 us (3%)
    pallas_call x1, Pallas kernels, slab_gradient(): pl.pallas_call(functools.partial(slab_kernel, bins, slabs), out_shape=jax...  57.2 us
    unnamed x1, local copies, waits for them, and re-layouts  1.54 us

profile of v3, /device:TPU:1, one launch (start us, length us, event | category | flops | bytes accessed | tf_op | source)
XLA Modules:
  0.0 58.7 jit_solution(516783039207809016)
XLA Ops:
  0.0 57.2 %shard_map.100 = f32[96,256]{1,0:T(8,128)} custom-call(bf16[32,2048]{1,0:T(8,128)(2,1)} %data_hbm.1, s32[1,32]{1,0:T(1,128)} %bitcast.10, s32[1,32]{1,0:T(1,128)} %bitcast.11, s32[1,32]{1,0:T(1,128)} %bitcast.12, s32[1,32]{1,0:T(1,128)} %bitcast.13, bf16[96,8192]{1,0:T(8,128)(2,1)} %sens_hbm.1, f32[96,256]{1,0:T(8,128)} %bitcast.8, f32[96,128]{1,0:T(8,128)} %bitcast.9, ...), custom_call_target="tpu_custom_call" | custom-call | tf_op jit(solution)/shard_map/pallas_call | solution.py:559
  57.2 1.5 %copy.12 = f32[1,96,256]{2,1,0:T(8,128)} copy(f32[1,96,256]{2,1,0:T(8,128)} %bitcast.7) | data formatting | bytes 196608

commit v4 on v3

--- a/solution.py
+++ b/solution.py
@@ -59,11 +59,16 @@
     return cos_out, sin_out
 
 
-def spline_weight(offset):
-    distance = jnp.abs(offset)
-    inside = 2.0 / 3.0 + distance * distance * (0.5 * distance - 1.0)
-    rest = jnp.maximum(2.0 - distance, 0.0)
-    return jnp.where(distance < 1.0, inside, rest * rest * (rest * (1.0 / 6.0)))
+def tap_weights(coord):
+    cell = jnp.floor(coord)
+    ahead = coord - cell
+    behind = 1.0 - ahead
+    return cell, [
+        behind * behind * behind * (1.0 / 6.0),
+        2.0 / 3.0 + ahead * ahead * (0.5 * ahead - 1.0),
+        2.0 / 3.0 + behind * behind * (0.5 * behind - 1.0),
+        ahead * ahead * ahead * (1.0 / 6.0),
+    ]
 
 
 def all_bytes(ref, sem):
@@ -138,7 +143,7 @@
     blocks = data.shape[0]
 
     barrier = pltpu.get_barrier_semaphore()
-    route_peers = [(side, step) for step in range(bins) for side in (1, 0)]
+    route_peers = [(side, step) for side in (0, 1) for step in (4, 5, 3, 6, 7, 1, 2, 0)]
     route_peers.remove((0, 0))
 
     def route_peer(across_half, step):
@@ -147,16 +152,20 @@
             "slab": opposite if across_half else slab,
         }
 
-    def half_peer(step):
-        return lax.rem(place + step, half_slabs)
+    half_order = [(dz, dy, dc) for dz in (0, 1) for dy in (2, 1, 3) for dc in (0, 1)]
+    half_order += [(1, 0, 0), (1, 0, 1), (0, 0, 1)]
+
+    def half_peer(dz, dy, dc):
+        z, y, core = lax.div(place, 8), lax.rem(lax.div(place, 2), 4), lax.rem(place, 2)
+        return 8 * lax.rem(z + dz, 2) + 2 * lax.rem(y + dy, 4) + lax.rem(core + dc, 2)
 
     for pair in route_peers:
         pl.semaphore_signal(barrier, inc=1, device_id=route_peer(*pair), device_id_type=MESH)
-    for step in range(1, half_slabs):
+    for hop in half_order:
         pl.semaphore_signal(
             barrier,
             inc=1,
-            device_id={"slab": half * half_slabs + half_peer(step)},
+            device_id={"slab": half * half_slabs + half_peer(*hop)},
             device_id_type=MESH,
         )
 
@@ -334,15 +343,7 @@
             base = pl.multiple_of((side * bins + source) * 8, 8)
             coord_x = coords_in[pl.ds(base + part, 1), :]
             coord_y = coords_in[pl.ds(base + KP + part, 1), :]
-            cell = jnp.floor(coord_y)
-            ahead = coord_y - cell
-            behind = 1.0 - ahead
-            weights = [
-                behind * behind * behind * (1.0 / 6.0),
-                2.0 / 3.0 + ahead * ahead * (0.5 * ahead - 1.0),
-                2.0 / 3.0 + behind * behind * (0.5 * behind - 1.0),
-                ahead * ahead * ahead * (1.0 / 6.0),
-            ]
+            cell, weights = tap_weights(coord_y)
             steps = y_offset * (cell - (1.0 + NG // 2))
             base_turns = steps * (1.0 / NG)
             base_cos, base_sin = turn_waves(base_turns - jnp.floor(base_turns))
@@ -355,14 +356,23 @@
             row_real[at, :] = sum_cos * base_cos - sum_sin * base_sin
             row_imag[at, :] = sum_cos * base_sin + sum_sin * base_cos
             lanes = pl.ds(pl.multiple_of(source * LANES, LANES), LANES)
-            turned = jnp.broadcast_to(coord_x, (LANES, LANES)).T
-            for first in range(0, NG, LANES):
-                cells = (iota((LANES, LANES), 1) + first).astype(F32)
-                across[lanes, first : first + LANES] = spline_weight(turned - cells).astype(BF16)
+            cell, weights = tap_weights(coord_x)
+            tile = (16, LANES)
+            weights = [jnp.broadcast_to(tap, tile).astype(BF16) for tap in weights]
+            for block in range(0, NG, LANES):
+                start = jnp.clip(cell - (1.0 + block), -8.0, LANES + 8.0)
+                away = (iota(tile, 0).astype(F32) - start).astype(BF16)
+                for first in range(0, LANES, tile[0]):
+                    value = jnp.zeros(tile, BF16)
+                    for tap, tap_weight in enumerate(weights):
+                        value = jnp.where(away == jnp.array(tap - first, BF16), tap_weight, value)
+                    across[block + first : block + first + tile[0], lanes] = value
             return carry
 
         lax.fori_loop(0, bins, prepare_source, 0)
-        kernel_x[step] = jnp.dot(across[...], x_table[...], preferred_element_type=F32).astype(BF16)
+        kernel_x[step] = lax.dot_general(
+            across[...], x_table[...], (((0,), (0,)), ((), ())), preferred_element_type=F32
+        ).astype(BF16)
         return carry
 
     lax.fori_loop(0, parts, prepare, 0)
@@ -410,7 +420,8 @@
         all_bytes(tiles_in.at[others], tile_recv_sems.at[part])
 
         def widen_samples(source, carry):
-            samples[source] = tiles_in[tile_rows(part * sources + source), :].astype(F32)
+            slot = part * sources + source
+            samples[slot] = tiles_in[tile_rows(slot), :].astype(F32)
             return carry
 
         lax.fori_loop(0, sources, widen_samples, 0)
@@ -429,8 +440,8 @@
                 for at_group, group in enumerate(groups):
                     for coil in range(GC):
                         row = group * GC + coil
-                        data_real = samples[side * bins + source, row : row + 1, :]
-                        data_imag = samples[side * bins + source, row + C : row + C + 1, :]
+                        data_real = samples[part * sources + side * bins + source, row : row + 1, :]
+                        data_imag = samples[part * sources + side * bins + source, row + C : row + C + 1, :]
                         first = at_group * group_rows + coil * WY
                         weighted[first : first + WY, lanes] = (
                             real * data_real - imag * data_imag
@@ -461,14 +472,9 @@
 
         lax.fori_loop(0, HALVES, one_side, 0)
 
-    for part in range(KP - 1):
-        take_tiles(part)
-        grid_part(part, tuple(range(COIL_GROUPS)))
-    take_tiles(KP - 1)
-    for group in range(COIL_GROUPS):
-        grid_part(KP - 1, (group,))
-        for step in range(1, half_slabs):
-            peer = half_peer(step)
+    def send_group(group):
+        for hop in half_order:
+            peer = half_peer(*hop)
             pltpu.make_async_remote_copy(
                 sending.at[group, peer],
                 received.at[group, place],
@@ -478,6 +484,20 @@
                 MESH,
             ).start()
         own_copy(group).start()
+
+    early = tuple(range(COIL_GROUPS // 2))
+    late = tuple(range(COIL_GROUPS // 2, COIL_GROUPS))
+    for part in range(KP - 1):
+        take_tiles(part)
+        grid_part(part, early)
+    take_tiles(KP - 1)
+    for group in early:
+        grid_part(KP - 1, (group,))
+        send_group(group)
+    for part in range(KP):
+        grid_part(part, late)
+    for group in late:
+        send_group(group)
 
     loads[8].wait()
     loads[9].wait()
@@ -572,10 +592,10 @@
             pltpu.VMEM(image.shape, F32),
             pltpu.VMEM(image.shape, F32),
             pltpu.VMEM(image.shape, F32),
-            pltpu.VMEM((sources, PC, LANES), F32),
+            pltpu.VMEM((KP * sources, PC, LANES), F32),
             pltpu.VMEM((parts * bins * WY, LANES), F32),
             pltpu.VMEM((parts * bins * WY, LANES), F32),
-            pltpu.VMEM((bins * LANES, NG), BF16),
+            pltpu.VMEM((NG, bins * LANES), BF16),
             pltpu.VMEM((parts, bins * LANES, 2 * NXI // HALVES), BF16),
             pltpu.VMEM((2 * C * WY, bins * LANES), BF16),
             pltpu.VMEM((2 * C * WY, 2 * NXI // HALVES), F32),

time: 59 us -> 58.2 us (0.986)
  Pallas kernels: 57.2 us -> 56.4 us
    pallas_call x1, Pallas kernels: 57.2 us -> 56.4 us  [slab_gradient(): pl.pallas_call(functools.partial(slab_kernel, bins, slabs), out_shape=jax...]
where the time goes in v4:
time: 58.2 us; the launch traced here: 57.9 us
  Pallas kernels  56.4 us (97%)
  local copies, waits for them, and re-layouts  1.54 us (3%)
    pallas_call x1, Pallas kernels, slab_gradient(): pl.pallas_call(functools.partial(slab_kernel, bins, slabs), out_shape=jax...  56.4 us
    unnamed x1, local copies, waits for them, and re-layouts  1.54 us

profile of v4, /device:TPU:1, one launch (start us, length us, event | category | flops | bytes accessed | tf_op | source)
XLA Modules:
  0.0 57.9 jit_solution(14825636057117235940)
XLA Ops:
  0.0 56.4 %shard_map.100 = f32[96,256]{1,0:T(8,128)} custom-call(bf16[32,2048]{1,0:T(8,128)(2,1)} %data_hbm.1, s32[1,32]{1,0:T(1,128)} %bitcast.10, s32[1,32]{1,0:T(1,128)} %bitcast.11, s32[1,32]{1,0:T(1,128)} %bitcast.12, s32[1,32]{1,0:T(1,128)} %bitcast.13, bf16[96,8192]{1,0:T(8,128)(2,1)} %sens_hbm.1, f32[96,256]{1,0:T(8,128)} %bitcast.8, f32[96,128]{1,0:T(8,128)} %bitcast.9, ...), custom_call_target="tpu_custom_call" | custom-call | tf_op jit(solution)/shard_map/pallas_call | solution.py:579
  56.4 1.5 %copy.12 = f32[1,96,256]{2,1,0:T(8,128)} copy(f32[1,96,256]{2,1,0:T(8,128)} %bitcast.7) | data formatting | bytes 196608

commit v5 on v4

--- a/solution.py
+++ b/solution.py
@@ -252,28 +252,6 @@
     )
     is_first = me == 0
     is_last = me == bins - 1
-    loads[5].wait()
-    pl.semaphore_wait(barrier, len(route_peers) + half_slabs - 1)
-
-    @pl.when(jnp.logical_not(is_first))
-    def _():
-        image_copy.start()
-
-    for pair in route_peers:
-        peer = route_peer(*pair)
-        pltpu.make_async_remote_copy(
-            coords.at[coord_rows(peer["bin"])],
-            coords_in.at[coord_rows(my_source)],
-            send_sems.at[0],
-            recv_sems.at[0],
-            peer,
-            MESH,
-        ).start()
-    own_coords = pltpu.make_async_copy(
-        coords.at[coord_rows(me)], coords_in.at[coord_rows(my_source)], own_sems.at[0]
-    )
-    own_coords.start()
-
     loads[4].wait()
     big = (bins * KP * 16, LANES)
     place_row = iota(big, 0)
@@ -304,6 +282,28 @@
         return carry
 
     lax.fori_loop(0, bins * KP // 2, turn_pair, 0)
+
+    loads[5].wait()
+    pl.semaphore_wait(barrier, len(route_peers) + half_slabs - 1)
+
+    @pl.when(jnp.logical_not(is_first))
+    def _():
+        image_copy.start()
+
+    for pair in route_peers:
+        peer = route_peer(*pair)
+        pltpu.make_async_remote_copy(
+            coords.at[coord_rows(peer["bin"])],
+            coords_in.at[coord_rows(my_source)],
+            send_sems.at[0],
+            recv_sems.at[0],
+            peer,
+            MESH,
+        ).start()
+    own_coords = pltpu.make_async_copy(
+        coords.at[coord_rows(me)], coords_in.at[coord_rows(my_source)], own_sems.at[0]
+    )
+    own_coords.start()
     own_tiles = []
     for part in range(KP):
         slot = part * sources + my_source
@@ -494,9 +494,9 @@
     for group in early:
         grid_part(KP - 1, (group,))
         send_group(group)
-    for part in range(KP):
-        grid_part(part, late)
     for group in late:
+        for part in range(KP):
+            grid_part(part, (group,))
         send_group(group)
 
     loads[8].wait()

time: 58.2 us -> 58.1 us (level)
  no operation moved by 1% of the time
where the time goes in v5:
time: 58.1 us; the launch traced here: 57.8 us
  Pallas kernels  56.3 us (97%)
  local copies, waits for them, and re-layouts  1.54 us (3%)
    pallas_call x1, Pallas kernels, slab_gradient(): pl.pallas_call(functools.partial(slab_kernel, bins, slabs), out_shape=jax...  56.3 us
    unnamed x1, local copies, waits for them, and re-layouts  1.54 us

profile of v5, /device:TPU:1, one launch (start us, length us, event | category | flops | bytes accessed | tf_op | source)
XLA Modules:
  0.0 57.8 jit_solution(7303696269377858663)
XLA Ops:
  0.0 56.3 %shard_map.100 = f32[96,256]{1,0:T(8,128)} custom-call(bf16[32,2048]{1,0:T(8,128)(2,1)} %data_hbm.1, s32[1,32]{1,0:T(1,128)} %bitcast.10, s32[1,32]{1,0:T(1,128)} %bitcast.11, s32[1,32]{1,0:T(1,128)} %bitcast.12, s32[1,32]{1,0:T(1,128)} %bitcast.13, bf16[96,8192]{1,0:T(8,128)(2,1)} %sens_hbm.1, f32[96,256]{1,0:T(8,128)} %bitcast.8, f32[96,128]{1,0:T(8,128)} %bitcast.9, ...), custom_call_target="tpu_custom_call" | custom-call | tf_op jit(solution)/shard_map/pallas_call | solution.py:579
  56.3 1.5 %copy.12 = f32[1,96,256]{2,1,0:T(8,128)} copy(f32[1,96,256]{2,1,0:T(8,128)} %bitcast.7) | data formatting | bytes 196608
